TPU v7x, 256 devices: a whole 4x4x8 slice. The times are simulated.
256 devices in a mesh: dp: 8 (over x, core), seq: 32 (over z, y).
Axes of the slice: x: 4, y: 4, z: 8, core: 2. Of those that a mesh axis runs over, the one named last changes fastest.
Arguments:
- query_blocks: bfloat16 [16, 2048, 4096], P('dp', 'seq'), may hold values from -64 to 64
- key_blocks: bfloat16 [16, 2048, 4096], P('dp', 'seq'), may hold values from -6 to 6
- value_blocks: bfloat16 [16, 2048, 4096], P('dp', 'seq'), may hold values from -6 to 6
- value_scales: float32 [16, 2048, 32], P('dp', 'seq'), may hold values from 0.25 to 4
- targets: bfloat16 [16, 2048, 4096], P('dp', 'seq'), may hold values from -41 to 41
- frame_ids: int32 [16, 2048], P('dp', 'seq'), may hold values from 0 to 15, never falling along the last dimension, each value on 1 to 256 neighbouring positions
- bucket_ids: int32 [16], P('dp'), may hold values from 0 to 7
Outputs:
- query_grad: bfloat16 [16, 2048, 4096], P('dp', 'seq')
- key_grad: bfloat16 [16, 2048, 4096], P('dp', 'seq')
- value_grad: bfloat16 [16, 2048, 4096], P('dp', 'seq')
Inputs may be any that keep to these rules, and one draw needn't show every extreme that they name: `frame_ids`: frame ids never fall along a sample; each frame holds 1 to 256 tokens.
All inputs are finite; a program needn't handle non-finite values.
Results may differ from a plain program's by a relative error of at most 0.009.
The roundings to bfloat16 on the way count: a program that leaves them out, or rounds other values in their place, can miss the bound.
Values may be sent and summed in bfloat16 or wider, within the bound.
A program may use at most 128 MiB of HBM per device.

v0:
```python
import jax
import jax.numpy as jnp
from jax import lax
from jax.sharding import PartitionSpec as P

HD = 128
LEN = 2048
NB = 8


def rotate(values, frame_ids, direction_sign):
    quarter = values.shape[-1] // 4
    inverse_freq = 10000.0 ** (-jnp.arange(quarter, dtype=jnp.float32) / quarter)
    angles = frame_ids.astype(jnp.float32)[..., None] * inverse_freq
    cosine = jnp.cos(angles)[..., None, :]
    sine_part = direction_sign * jnp.sin(angles)[..., None, :]
    first_half = values[..., :quarter]
    second_half = values[..., quarter : 2 * quarter]
    return jnp.concatenate(
        [
            first_half * cosine - second_half * sine_part,
            first_half * sine_part + second_half * cosine,
            values[..., 2 * quarter :],
        ],
        axis=-1,
    )


def split_heads(rows):
    return rows.reshape(rows.shape[0], rows.shape[1] // HD, HD)


def softmax_parts(query_rows, key_rows):
    scores = jnp.einsum(
        "qhd,khd->hqk", query_rows, key_rows, preferred_element_type=jnp.float32
    ) * HD ** (-0.5)
    row_max = jnp.max(scores, axis=-1, keepdims=True)
    exp_scores = jnp.exp(scores - row_max)
    row_total = jnp.sum(exp_scores, axis=-1, keepdims=True)
    return (scores, row_max, row_total, exp_scores / row_total)


def grads_from(probs_full, query_rows, key_rows, value_rows, attended, cotangent):
    length = query_rows.shape[0]
    probs_low = probs_full.astype(jnp.bfloat16)
    grad_value = jnp.einsum(
        "hqk,qhd->khd", probs_low, cotangent, preferred_element_type=jnp.float32
    )
    grad_probs = jnp.einsum(
        "qhd,khd->hqk", cotangent, value_rows, preferred_element_type=jnp.float32
    )
    row_delta = jnp.transpose(
        jnp.sum(cotangent.astype(jnp.float32) * attended.astype(jnp.float32), axis=-1)
    )[:, :, None]
    grad_scores = (probs_full * (grad_probs - row_delta) * HD ** (-0.5)).astype(jnp.bfloat16)
    grad_query = jnp.einsum(
        "hqk,khd->qhd", grad_scores, key_rows, preferred_element_type=jnp.float32
    )
    grad_key = jnp.einsum(
        "hqk,qhd->khd", grad_scores, query_rows, preferred_element_type=jnp.float32
    )
    return (
        grad_query.astype(jnp.bfloat16).reshape(length, -1),
        grad_key.astype(jnp.bfloat16).reshape(length, -1),
        grad_value.astype(jnp.bfloat16).reshape(length, -1),
    )


def forward_item(pieces):
    query_rows, key_rows, value_rows = [split_heads(piece) for piece in pieces]
    scores, row_max, row_total, probs_full = softmax_parts(query_rows, key_rows)
    attended = jnp.einsum(
        "hqk,khd->qhd",
        probs_full.astype(jnp.bfloat16),
        value_rows,
        preferred_element_type=jnp.float32,
    ).astype(jnp.bfloat16)
    return (attended.reshape(query_rows.shape[0], -1), row_max, row_total)


def backward_item(pieces):
    query_in, key_in, value_in, attended, cotangent, row_max, row_total = pieces
    query_rows = split_heads(query_in)
    key_rows = split_heads(key_in)
    scores = jnp.einsum(
        "qhd,khd->hqk", query_rows, key_rows, preferred_element_type=jnp.float32
    ) * HD ** (-0.5)
    probs_full = jnp.exp(scores - row_max) / row_total
    return grads_from(
        probs_full,
        query_rows,
        key_rows,
        split_heads(value_in),
        split_heads(attended),
        split_heads(cotangent),
    )


def local(query_blocks, key_blocks, value_blocks, value_scales, targets, frame_ids, bucket_ids):
    samples_here, tokens_here, width = query_blocks.shape
    head_count = value_scales.shape[2]
    shaped = (samples_here, tokens_here, head_count, HD)
    query_rot = rotate(query_blocks.astype(jnp.float32).reshape(shaped), frame_ids, 1.0)
    query_rot = query_rot.astype(jnp.bfloat16).reshape(samples_here, tokens_here, width)
    key_rot = rotate(key_blocks.astype(jnp.float32).reshape(shaped), frame_ids, 1.0)
    key_rot = key_rot.astype(jnp.bfloat16).reshape(samples_here, tokens_here, width)
    value_deq = value_blocks.astype(jnp.float32).reshape(shaped) * value_scales[..., None]
    value_deq = value_deq.astype(jnp.bfloat16).reshape(samples_here, tokens_here, width)
    query_heads, key_heads, value_heads = (
        lax.all_to_all(query_rot, "seq", split_axis=2, concat_axis=1, tiled=True),
        lax.all_to_all(key_rot, "seq", split_axis=2, concat_axis=1, tiled=True),
        lax.all_to_all(value_deq, "seq", split_axis=2, concat_axis=1, tiled=True),
    )
    attended, row_max, row_total = lax.map(forward_item, (query_heads, key_heads, value_heads))
    attended_tokens = lax.all_to_all(attended, "seq", split_axis=1, concat_axis=2, tiled=True)
    errors = attended_tokens.astype(jnp.float32) - targets.astype(jnp.float32)
    loss_part = jnp.sum(errors * errors, axis=(1, 2)) / (LEN * width)
    cotangent = lax.all_to_all(
        errors.astype(jnp.bfloat16), "seq", split_axis=2, concat_axis=1, tiled=True
    )
    grad_query, grad_key, grad_value = lax.map(
        backward_item,
        (query_heads, key_heads, value_heads, attended, cotangent, row_max, row_total),
    )
    grad_query, grad_key, grad_value = (
        lax.all_to_all(grad_query, "seq", split_axis=1, concat_axis=2, tiled=True),
        lax.all_to_all(grad_key, "seq", split_axis=1, concat_axis=2, tiled=True),
        lax.all_to_all(grad_value, "seq", split_axis=1, concat_axis=2, tiled=True),
    )
    first_device = (lax.axis_index("seq") == 0).astype(jnp.float32)
    onehot = (bucket_ids[:, None] == jnp.arange(NB, dtype=jnp.int32)[None, :]).astype(jnp.float32)
    bucket_loss, bucket_count = lax.psum(
        (jnp.sum(onehot * loss_part[:, None], axis=0), jnp.sum(onehot, axis=0) * first_device),
        ("dp", "seq"),
    )
    mean_all = jnp.sum(bucket_loss) / jnp.sum(bucket_count)
    chosen_loss = jnp.sum(onehot * bucket_loss[None, :], axis=1)
    chosen_count = jnp.sum(onehot * bucket_count[None, :], axis=1)
    weight = mean_all / (chosen_loss / chosen_count + 1e-05)
    scaled = weight[:, None, None, None]
    query_grad = scaled * rotate(grad_query.astype(jnp.float32).reshape(shaped), frame_ids, -1.0)
    key_grad = scaled * rotate(grad_key.astype(jnp.float32).reshape(shaped), frame_ids, -1.0)
    value_grad = scaled * grad_value.astype(jnp.float32).reshape(shaped) * value_scales[..., None]
    out_shape = (samples_here, tokens_here, width)
    return (
        query_grad.astype(jnp.bfloat16).reshape(out_shape),
        key_grad.astype(jnp.bfloat16).reshape(out_shape),
        value_grad.astype(jnp.bfloat16).reshape(out_shape),
    )


def solution(mesh):
    return jax.shard_map(
        local,
        mesh=mesh,
        in_specs=(
            P("dp", "seq", None),
            P("dp", "seq", None),
            P("dp", "seq", None),
            P("dp", "seq", None),
            P("dp", "seq", None),
            P("dp", "seq"),
            P("dp"),
        ),
        out_specs=(P("dp", "seq", None), P("dp", "seq", None), P("dp", "seq", None)),
        check_vma=False,
    )
```

profile of v0, /device:TPU:1, one launch (start us, length us, event | category | flops | bytes accessed | tf_op | source)
XLA Modules:
  0.0 499.8 jit_solution(16877208844494405980)
XLA Ops:
  3.6 2.1 multiply_convert_fusion.3
  5.7 2.8 copy.64
  8.6 2.2 reshape.236
  10.8 12.2 %all-to-all-start = ((bf16[32,2,8192]{2,1,0:T(2,128)(2,1)}), bf16[32,2,8192]{2,1,0:T(2,128)(2,1)S(1)}, u32[]{:S(2)}, u32[]{:S(2)}) async-start(bf16[32,2,8192]{2,1,0:T(2,128)(2,1)} %reshape.236), calls=%async_computation | async-start | bytes 2097152 | tf_op jit(solution)/shard_map/all_to_all | solution.py:112
  27.3 3.2 pad_maximum_fusion.2
  30.5 3.4 copy.87
  33.9 2.2 reshape.234
  36.1 13.1 %all-to-all-done = bf16[32,2,8192]{2,1,0:T(2,128)(2,1)S(1)} async-done(((bf16[32,2,8192]{2,1,0:T(2,128)(2,1)}), bf16[32,2,8192]{2,1,0:T(2,128)(2,1)S(1)}, u32[]{:S(2)}, u32[]{:S(2)}) %all-to-all-start) | async-done | bytes 1048608 | tf_op jit(solution)/shard_map/all_to_all | solution.py:112
  49.2 6.5 %all-to-all-start.1 = ((bf16[32,2,8192]{2,1,0:T(2,128)(2,1)}), bf16[32,2,8192]{2,1,0:T(2,128)(2,1)}, u32[]{:S(2)}, u32[]{:S(2)}) async-start(bf16[32,2,8192]{2,1,0:T(2,128)(2,1)} %reshape.234), calls=%async_computation.1 | async-start | bytes 2097152 | tf_op jit(solution)/shard_map/all_to_all | solution.py:110
  55.7 3.4 copy.90
  59.1 2.2 reshape.232
  61.3 19.6 %all-to-all-done.1 = bf16[32,2,8192]{2,1,0:T(2,128)(2,1)} async-done(((bf16[32,2,8192]{2,1,0:T(2,128)(2,1)}), bf16[32,2,8192]{2,1,0:T(2,128)(2,1)}, u32[]{:S(2)}, u32[]{:S(2)}) %all-to-all-start.1) | async-done | bytes 1048608 | tf_op jit(solution)/shard_map/all_to_all | solution.py:110
  81.0 7.1 %all-to-all-start.2 = ((bf16[32,2,8192]{2,1,0:T(2,128)(2,1)}), bf16[32,2,8192]{2,1,0:T(2,128)(2,1)}, u32[]{:S(2)}, u32[]{:S(2)}) async-start(bf16[32,2,8192]{2,1,0:T(2,128)(2,1)} %reshape.232), calls=%async_computation.2 | async-start | bytes 2097152 | tf_op jit(solution)/shard_map/all_to_all | solution.py:111
  89.5 3.9 copy.65
  93.3 5.0 %reshape.235 = bf16[4096,2,64]{2,1,0:T(2,128)(2,1)S(1)} reshape(bf16[32,2,8192]{2,1,0:T(2,128)(2,1)} %all-to-all-done.1) | data formatting | bytes 2097152
  98.3 2.8 copy.89
  101.2 11.3 %all-to-all-done.2 = bf16[32,2,8192]{2,1,0:T(2,128)(2,1)} async-done(((bf16[32,2,8192]{2,1,0:T(2,128)(2,1)}), bf16[32,2,8192]{2,1,0:T(2,128)(2,1)}, u32[]{:S(2)}, u32[]{:S(2)}) %all-to-all-start.2) | async-done | bytes 1048608 | tf_op jit(solution)/shard_map/all_to_all | solution.py:111
  112.5 5.7 %reshape.233 = bf16[4096,2,64]{2,1,0:T(2,128)(2,1)} reshape(bf16[32,2,8192]{2,1,0:T(2,128)(2,1)} %all-to-all-done.2) | data formatting | bytes 2097152
  118.2 4.9 copy.92
  123.2 49.3 %while.28 = (s32[]{:T(128)}, bf16[2,2048,128]{1,2,0:T(8,128)(2,1)S(1)}, f32[2,1,2048,1]{2,3,1,0:T(1,128)S(1)}, f32[2,1,2048,1]{2,3,1,0:T(1,128)S(1)}, bf16[2,204...) while((s32[]{:T(128)}, ...), condition=%wide.region_3.4_spmd, body=%wide.region_0.3_spmd.sunk | while | flops 2185490432 | bytes 56699004 | solution.py:114
  123.2 8.1 %multiply_reduce_fusion.5 = (f32[2048]{0:T(1024)S(1)}, f32[2048,2048]{0,1:T(8,128)}) fusion(bf16[2,2048,128]{2,1,0:T(8,128)(2,1)S(1)} %get-tuple-element.375, s32[]{:T(128)S(6)} %copy.121, bf16[2,2048,128]{2,1,0:T(8,128)(2,1)S(1)} %get-tuple-element.374), kind=kOutput, calls=%fused_computation.2.clone.1 | convolution fusion | flops 1082128384 | bytes 17835008 | tf_op jit(solution)/shard_map/while/body/eval_jaxpr/qhd,khd->hqk/dot_general | solution.py:34
  131.3 8.6 %fusion.74 = f32[2048]{0:T(1024)S(1)} fusion(f32[2048,2048]{0,1:T(8,128)} %get-tuple-element.336, f32[2048]{0:T(1024)S(1)} %get-tuple-element.337), kind=kLoop, calls=%fused_computation.3.clone.1 | loop fusion | flops 12580864 | bytes 16793600 | tf_op jit(solution)/shard_map/while/body/eval_jaxpr/reduce_sum | solution.py:39
  139.9 7.8 %fusion.75 = bf16[2,2048,128]{1,2,0:T(8,128)(2,1)S(1)} fusion(bf16[2,2048,128]{1,2,0:T(8,128)(2,1)S(1)} %get-tuple-element.362, s32[]{:T(128)S(6)} %copy.121, f32[2048,2048]{0,1:T(8,128)} %get-tuple-element.336, f32[2048]{0:T(1024)S(1)} %fusion.74, f32[2048]{0:T(1024)S(1)} %get-tuple-element.337, bf16[2,2048,128]{2,1,0:T(8,128)(2,1)S(1)} %copy-done.7), kind=kOutput, calls=%fused_computation.7.clone.1 | convolution fusion | flops 1090781184 | bytes 17843200 | tf_op jit(solution)/shard_map/while/body/eval_jaxpr/hqk,khd->qhd/dot_general | solution.py:72
  147.8 8.1 %multiply_reduce_fusion.5 = (f32[2048]{0:T(1024)S(1)}, f32[2048,2048]{0,1:T(8,128)}) fusion(bf16[2,2048,128]{2,1,0:T(8,128)(2,1)S(1)} %get-tuple-element.375, s32[]{:T(128)S(6)} %copy.121, bf16[2,2048,128]{2,1,0:T(8,128)(2,1)S(1)} %get-tuple-element.374), kind=kOutput, calls=%fused_computation.2.clone.1 | convolution fusion | flops 1082128384 | bytes 17835008 | tf_op jit(solution)/shard_map/while/body/eval_jaxpr/qhd,khd->hqk/dot_general | solution.py:34
  155.9 8.6 %fusion.74 = f32[2048]{0:T(1024)S(1)} fusion(f32[2048,2048]{0,1:T(8,128)} %get-tuple-element.336, f32[2048]{0:T(1024)S(1)} %get-tuple-element.337), kind=kLoop, calls=%fused_computation.3.clone.1 | loop fusion | flops 12580864 | bytes 16793600 | tf_op jit(solution)/shard_map/while/body/eval_jaxpr/reduce_sum | solution.py:39
  164.6 7.8 %fusion.75 = bf16[2,2048,128]{1,2,0:T(8,128)(2,1)S(1)} fusion(bf16[2,2048,128]{1,2,0:T(8,128)(2,1)S(1)} %get-tuple-element.362, s32[]{:T(128)S(6)} %copy.121, f32[2048,2048]{0,1:T(8,128)} %get-tuple-element.336, f32[2048]{0:T(1024)S(1)} %fusion.74, f32[2048]{0:T(1024)S(1)} %get-tuple-element.337, bf16[2,2048,128]{2,1,0:T(8,128)(2,1)S(1)} %copy-done.7), kind=kOutput, calls=%fused_computation.7.clone.1 | convolution fusion | flops 1090781184 | bytes 17843200 | tf_op jit(solution)/shard_map/while/body/eval_jaxpr/hqk,khd->qhd/dot_general | solution.py:72
  172.5 2.4 copy.72
  174.9 32.4 %all_to_all.108 = bf16[2,2048,128]{2,0,1:T(2,128)(2,1)S(1)} all-to-all(bf16[2,2048,128]{2,0,1:T(2,128)(2,1)} %copy.72), channel_id=1, replica_groups=mesh['dp'=8,'seq'=32] {'seq'}, dimensions={1} | all-to-all | bytes 2097152 | tf_op jit(solution)/shard_map/all_to_all | solution.py:115
  207.4 2.1 multiply_reduce_fusion.2
  209.5 5.5 %copy.75 = bf16[2,64,4096]{1,0,2:T(2,128)(2,1)} copy(bf16[2,64,4096]{2,1,0:T(8,128)(2,1)} %get-tuple-element.211) | data formatting | bytes 2097152 | tf_op jit(solution)/shard_map/convert_element_type | solution.py:119
  215.0 5.8 %reshape.238 = bf16[32,2,8192]{2,1,0:T(2,128)(2,1)} reshape(bf16[4096,2,64]{2,1,0:T(2,128)(2,1)} %bitcast.211) | data formatting | bytes 2097152
  220.8 6.5 %all-to-all-start.4 = ((bf16[32,2,8192]{2,1,0:T(2,128)(2,1)}), bf16[32,2,8192]{2,1,0:T(2,128)(2,1)S(1)}, u32[]{:S(2)}, u32[]{:S(2)}) async-start(bf16[32,2,8192]{2,1,0:T(2,128)(2,1)} %reshape.238), calls=%async_computation.4 | async-start | bytes 2097152 | tf_op jit(solution)/shard_map/all_to_all | solution.py:118
  227.3 24.3 %all-to-all-done.4 = bf16[32,2,8192]{2,1,0:T(2,128)(2,1)S(1)} async-done(((bf16[32,2,8192]{2,1,0:T(2,128)(2,1)}), bf16[32,2,8192]{2,1,0:T(2,128)(2,1)S(1)}, u32[]{:S(2)}, u32[]{:S(2)}) %all-to-all-start.4) | async-done | bytes 1048608 | tf_op jit(solution)/shard_map/all_to_all | solution.py:118
  251.6 2.3 reshape.239
  253.9 4.9 copy.76
  262.1 57.3 %while.29 = (s32[]{:T(128)}, bf16[2,2048,128]{1,2,0:T(8,128)(2,1)}, bf16[2,2048,128]{1,2,0:T(8,128)(2,1)}, bf16[2,2048,128]{1,2,0:T(8,128)(2,1)}, bf16[2,2048,12...) while((s32[]{:T(128)}, bf16[2,2048,128]{1,2,0:T(8,128)(2,1)}, ...), condition=%wide.region_15.16_spmd, body=%wide.region_13.15_spmd.sunk | while | flops 5404096512 | bytes 176231760 | solution.py:121
  264.8 4.8 exponential_divide_fusion.2
  269.6 5.7 %copy-done = f32[2048,2048]{1,0:T(8,128)} copy-done((f32[2048,2048]{1,0:T(8,128)}, f32[2048,2048]{1,0:T(8,128)S(1)}, u32[]{:S(2)}) %copy-start) | copy-done | bytes 16777240 | tf_op jit(solution)/shard_map/while
  275.3 2.1 fusion.88
  277.4 7.3 %multiply_convert_fusion.5 = bf16[2048,2048]{1,0:T(8,128)(2,1)S(1)} fusion(f32[2048,2048]{1,0:T(8,128)} %copy-done, f32[2048]{0:T(1024)S(1)} %multiply_reduce_fusion.6, bf16[2,2048,128]{2,1,0:T(8,128)(2,1)} %get-tuple-element.410, s32[]{:T(128)S(6)} %copy.133, bf16[2,2048,128]{2,1,0:T(8,128)(2,1)S(1)} %get-tuple-element.409), kind=kOutput, calls=%fused_computation.20.clone.1 | convolution fusion | flops 1090519040 | bytes 26223616 | tf_op jit(solution)/shard_map/while/body/eval_jaxpr/qhd,khd->hqk/dot_general | solution.py:49
  284.8 2.1 fusion.87
  286.9 2.9 fusion.86
  293.5 4.8 exponential_divide_fusion.2
  298.3 5.7 %copy-done = f32[2048,2048]{1,0:T(8,128)} copy-done((f32[2048,2048]{1,0:T(8,128)}, f32[2048,2048]{1,0:T(8,128)S(1)}, u32[]{:S(2)}) %copy-start) | copy-done | bytes 16777240 | tf_op jit(solution)/shard_map/while
  304.0 2.1 fusion.88
  306.1 7.3 %multiply_convert_fusion.5 = bf16[2048,2048]{1,0:T(8,128)(2,1)S(1)} fusion(f32[2048,2048]{1,0:T(8,128)} %copy-done, f32[2048]{0:T(1024)S(1)} %multiply_reduce_fusion.6, bf16[2,2048,128]{2,1,0:T(8,128)(2,1)} %get-tuple-element.410, s32[]{:T(128)S(6)} %copy.133, bf16[2,2048,128]{2,1,0:T(8,128)(2,1)S(1)} %get-tuple-element.409), kind=kOutput, calls=%fused_computation.20.clone.1 | convolution fusion | flops 1090519040 | bytes 26223616 | tf_op jit(solution)/shard_map/while/body/eval_jaxpr/qhd,khd->hqk/dot_general | solution.py:49
  313.4 2.1 fusion.87
  315.5 2.9 fusion.86
  319.4 3.8 copy.78
  323.2 6.6 %all-to-all-start.5 = ((bf16[2,2048,128]{2,0,1:T(2,128)(2,1)}), bf16[2,2048,128]{2,0,1:T(2,128)(2,1)S(1)}, u32[]{:S(2)}, u32[]{:S(2)}) async-start(bf16[2,2048,128]{2,0,1:T(2,128)(2,1)} %copy.78), calls=%async_computation.5 | async-start | bytes 2097152 | tf_op jit(solution)/shard_map/all_to_all | solution.py:126
  329.8 2.0 copy.81
  331.8 21.9 %all-to-all-done.5 = bf16[2,2048,128]{2,0,1:T(2,128)(2,1)S(1)} async-done(((bf16[2,2048,128]{2,0,1:T(2,128)(2,1)}), bf16[2,2048,128]{2,0,1:T(2,128)(2,1)S(1)}, u32[]{:S(2)}, u32[]{:S(2)}) %all-to-all-start.5) | async-done | bytes 1048608 | tf_op jit(solution)/shard_map/all_to_all | solution.py:126
  353.6 6.6 %all-to-all-start.6 = ((bf16[2,2048,128]{2,0,1:T(2,128)(2,1)}), bf16[2,2048,128]{2,0,1:T(2,128)(2,1)S(1)}, u32[]{:S(2)}, u32[]{:S(2)}) async-start(bf16[2,2048,128]{2,0,1:T(2,128)(2,1)} %copy.81), calls=%async_computation.6 | async-start | bytes 2097152 | tf_op jit(solution)/shard_map/all_to_all | solution.py:127
  360.3 3.7 copy.84
  364.0 19.8 %all-to-all-done.6 = bf16[2,2048,128]{2,0,1:T(2,128)(2,1)S(1)} async-done(((bf16[2,2048,128]{2,0,1:T(2,128)(2,1)}), bf16[2,2048,128]{2,0,1:T(2,128)(2,1)S(1)}, u32[]{:S(2)}, u32[]{:S(2)}) %all-to-all-start.6) | async-done | bytes 1048608 | tf_op jit(solution)/shard_map/all_to_all | solution.py:127
  383.8 6.6 %all-to-all-start.7 = ((bf16[2,2048,128]{2,0,1:T(2,128)(2,1)}), bf16[2,2048,128]{2,0,1:T(2,128)(2,1)S(1)}, u32[]{:S(2)}, u32[]{:S(2)}) async-start(bf16[2,2048,128]{2,0,1:T(2,128)(2,1)} %copy.84), calls=%async_computation.7 | async-start | bytes 2097152 | tf_op jit(solution)/shard_map/all_to_all | solution.py:128
  390.5 82.2 %all-reduce = (f32[8]{0:T(128)S(1)}, f32[8]{0:T(128)S(1)}) all-reduce(f32[8]{0:T(128)S(1)} %broadcast_multiply_fusion.1, f32[8]{0:T(128)S(1)} %get-tuple-element.165), channel_id=1, replica_groups=mesh['dp'=8,'seq'=32] {'dp','seq'}, use_global_device_ids=true, to_apply=%region_9.10 | all-reduce | flops 16 | bytes 128 | tf_op jit(solution)/shard_map/psum | solution.py:132
  477.0 2.0 slice.61
  479.8 3.2 multiply_subtract_fusion
  483.0 2.5 pad_maximum_fusion
  485.5 1.7 concatenate.21
  487.3 5.4 %pad_maximum_fusion.1 = f32[2,64,32,128]{3,2,1,0:T(8,128)} fusion(f32[2,64,32,64]{3,2,1,0:T(8,128)} %slice.61, f32[2,64,32,32]{3,2,1,0:T(8,128)} %get-tuple-element.213, f32[2,64,32,32]{3,2,1,0:T(8,128)} %get-tuple-element.212), kind=kLoop, calls=%fused_computation.58 | loop fusion | flops 1048576 | bytes 4194304 | tf_op jit(solution)/shard_map/concatenate | solution.py:19
  492.6 2.8 concatenate.23
  497.6 1.7 multiply_convert_fusion.1
  (104 shorter events, 25.6 us)
Async XLA Ops:
  8.6 14.4 %copy-start.20 = (s32[2,64]{1,0:T(2,128)S(1)}, s32[2,64]{1,0:T(2,128)}, u32[]{:S(2)}) copy-start(s32[2,64]{1,0:T(2,128)} %param.16) | copy-start | bytes 1540
  10.8 12.2 %copy-start.12 = (bf16[2,64,4096]{2,1,0:T(8,128)(2,1)S(1)}, bf16[2,64,4096]{2,1,0:T(8,128)(2,1)}, u32[]{:S(2)}) copy-start(bf16[2,64,4096]{2,1,0:T(8,128)(2,1)} %param.11) | copy-start | bytes 3145732
  10.8 12.5 %copy-start.13 = (bf16[2,64,4096]{2,1,0:T(8,128)(2,1)S(1)}, bf16[2,64,4096]{2,1,0:T(8,128)(2,1)}, u32[]{:S(2)}) copy-start(bf16[2,64,4096]{2,1,0:T(8,128)(2,1)} %param.12) | copy-start | bytes 3145732
  10.8 38.4 %all-to-all-start = ((bf16[32,2,8192]{2,1,0:T(2,128)(2,1)}), bf16[32,2,8192]{2,1,0:T(2,128)(2,1)S(1)}, u32[]{:S(2)}, u32[]{:S(2)}) async-start(bf16[32,2,8192]{2,1,0:T(2,128)(2,1)} %reshape.236), calls=%async_computation | async-start | bytes 2097152 | tf_op jit(solution)/shard_map/all_to_all | solution.py:112
  25.2 0.6 copy-start.15
  49.2 31.8 %all-to-all-start.1 = ((bf16[32,2,8192]{2,1,0:T(2,128)(2,1)}), bf16[32,2,8192]{2,1,0:T(2,128)(2,1)}, u32[]{:S(2)}, u32[]{:S(2)}) async-start(bf16[32,2,8192]{2,1,0:T(2,128)(2,1)} %reshape.234), calls=%async_computation.1 | async-start | bytes 2097152 | tf_op jit(solution)/shard_map/all_to_all | solution.py:110
  81.0 31.5 %all-to-all-start.2 = ((bf16[32,2,8192]{2,1,0:T(2,128)(2,1)}), bf16[32,2,8192]{2,1,0:T(2,128)(2,1)}, u32[]{:S(2)}, u32[]{:S(2)}) async-start(bf16[32,2,8192]{2,1,0:T(2,128)(2,1)} %reshape.232), calls=%async_computation.2 | async-start | bytes 2097152 | tf_op jit(solution)/shard_map/all_to_all | solution.py:111
  131.3 8.6 %copy-start.7 = (bf16[2,2048,128]{2,1,0:T(8,128)(2,1)S(1)}, bf16[2,2048,128]{2,1,0:T(8,128)(2,1)}, u32[]{:S(2)}) copy-start(bf16[2,2048,128]{2,1,0:T(8,128)(2,1)} %get-tuple-element.373) | copy-start | bytes 3145732 | tf_op jit(solution)/shard_map/while
  155.9 8.6 %copy-start.7 = (bf16[2,2048,128]{2,1,0:T(8,128)(2,1)S(1)}, bf16[2,2048,128]{2,1,0:T(8,128)(2,1)}, u32[]{:S(2)}) copy-start(bf16[2,2048,128]{2,1,0:T(8,128)(2,1)} %get-tuple-element.373) | copy-start | bytes 3145732 | tf_op jit(solution)/shard_map/while
  172.4 42.5 %copy-start.1 = (bf16[2,2048,128]{2,1,0:T(8,128)(2,1)}, bf16[2,2048,128]{2,1,0:T(8,128)(2,1)S(1)}, u32[]{:S(2)}) copy-start(bf16[2,2048,128]{2,1,0:T(8,128)(2,1)S(1)} %get-tuple-element.413) | copy-start | bytes 3145732
  172.5 42.5 %copy-start.3 = (bf16[2,2048,128]{2,1,0:T(8,128)(2,1)}, bf16[2,2048,128]{2,1,0:T(8,128)(2,1)S(1)}, u32[]{:S(2)}) copy-start(bf16[2,2048,128]{2,1,0:T(8,128)(2,1)S(1)} %get-tuple-element.414) | copy-start | bytes 3145732
  174.9 32.5 %copy-start.14 = (bf16[2,64,4096]{2,1,0:T(8,128)(2,1)S(1)}, bf16[2,64,4096]{2,1,0:T(8,128)(2,1)}, u32[]{:S(2)}) copy-start(bf16[2,64,4096]{2,1,0:T(8,128)(2,1)} %param.15) | copy-start | bytes 3145732
  220.8 30.8 %all-to-all-start.4 = ((bf16[32,2,8192]{2,1,0:T(2,128)(2,1)}), bf16[32,2,8192]{2,1,0:T(2,128)(2,1)S(1)}, u32[]{:S(2)}, u32[]{:S(2)}) async-start(bf16[32,2,8192]{2,1,0:T(2,128)(2,1)} %reshape.238), calls=%async_computation.4 | async-start | bytes 2097152 | tf_op jit(solution)/shard_map/all_to_all | solution.py:118
  262.1 1.0 copy-start.5
  269.6 5.7 %copy-start = (f32[2048,2048]{1,0:T(8,128)}, f32[2048,2048]{1,0:T(8,128)S(1)}, u32[]{:S(2)}) copy-start(f32[2048,2048]{1,0:T(8,128)S(1)} %exponential_divide_fusion.2) | copy-start | bytes 50331652 | tf_op jit(solution)/shard_map/while
  277.4 7.3 %copy-start.2 = (bf16[2,2048,128]{2,1,0:T(8,128)(2,1)S(1)}, bf16[2,2048,128]{2,1,0:T(8,128)(2,1)}, u32[]{:S(2)}) copy-start(bf16[2,2048,128]{2,1,0:T(8,128)(2,1)} %get-tuple-element.406) | copy-start | bytes 3145732 | tf_op jit(solution)/shard_map/while
  284.8 2.1 copy-start.4
  284.8 2.1 copy-start.10
  286.9 3.9 copy-start.6
  289.8 1.0 copy-start.11
  290.8 1.0 copy-start.5
  298.3 5.7 %copy-start = (f32[2048,2048]{1,0:T(8,128)}, f32[2048,2048]{1,0:T(8,128)S(1)}, u32[]{:S(2)}) copy-start(f32[2048,2048]{1,0:T(8,128)S(1)} %exponential_divide_fusion.2) | copy-start | bytes 50331652 | tf_op jit(solution)/shard_map/while
  306.1 7.3 %copy-start.2 = (bf16[2,2048,128]{2,1,0:T(8,128)(2,1)S(1)}, bf16[2,2048,128]{2,1,0:T(8,128)(2,1)}, u32[]{:S(2)}) copy-start(bf16[2,2048,128]{2,1,0:T(8,128)(2,1)} %get-tuple-element.406) | copy-start | bytes 3145732 | tf_op jit(solution)/shard_map/while
  313.4 2.1 copy-start.4
  313.4 2.1 copy-start.10
  315.5 3.9 copy-start.6
  318.4 1.0 copy-start.11
  319.4 10.3 %copy-start.9 = (bf16[2,2048,128]{1,2,0:T(8,128)(2,1)S(1)}, bf16[2,2048,128]{1,2,0:T(8,128)(2,1)}, u32[]{:S(2)}) copy-start(bf16[2,2048,128]{1,2,0:T(8,128)(2,1)} %get-tuple-element.105) | copy-start | bytes 3145732
  323.2 30.4 %all-to-all-start.5 = ((bf16[2,2048,128]{2,0,1:T(2,128)(2,1)}), bf16[2,2048,128]{2,0,1:T(2,128)(2,1)S(1)}, u32[]{:S(2)}, u32[]{:S(2)}) async-start(bf16[2,2048,128]{2,0,1:T(2,128)(2,1)} %copy.78), calls=%async_computation.5 | async-start | bytes 2097152 | tf_op jit(solution)/shard_map/all_to_all | solution.py:126
  353.6 30.1 %all-to-all-start.6 = ((bf16[2,2048,128]{2,0,1:T(2,128)(2,1)}), bf16[2,2048,128]{2,0,1:T(2,128)(2,1)S(1)}, u32[]{:S(2)}, u32[]{:S(2)}) async-start(bf16[2,2048,128]{2,0,1:T(2,128)(2,1)} %copy.81), calls=%async_computation.6 | async-start | bytes 2097152 | tf_op jit(solution)/shard_map/all_to_all | solution.py:127
  360.3 30.1 %copy-start.21 = (f32[2]{0:T(128)S(1)}, f32[2]{0:T(128)}, u32[]{:S(2)}) copy-start(f32[2]{0:T(128)} %get-tuple-element.210) | copy-start | bytes 28
  360.3 30.1 %copy-start.19 = (s32[2]{0:T(128)S(1)}, s32[2]{0:T(128)}, u32[]{:S(2)}) copy-start(s32[2]{0:T(128)} %param.17) | copy-start | bytes 28
  383.8 111.6 %all-to-all-start.7 = ((bf16[2,2048,128]{2,0,1:T(2,128)(2,1)}), bf16[2,2048,128]{2,0,1:T(2,128)(2,1)S(1)}, u32[]{:S(2)}, u32[]{:S(2)}) async-start(bf16[2,2048,128]{2,0,1:T(2,128)(2,1)} %copy.84), calls=%async_computation.7 | async-start | bytes 2097152 | tf_op jit(solution)/shard_map/all_to_all | solution.py:128
  478.9 0.8 copy-start.16
  478.9 0.9 copy-start.17
  495.4 0.8 copy-start.18
  495.4 2.2 copy-start.8
where the time goes:
time: 509 us; the launch traced here: 500 us
  blocking collectives  115 us (23%)
  waiting for transfers between devices  110 us (22%)
  local copies, waits for them, and re-layouts  106 us (21%)
  matrix products  70.2 us (14%)
  starting transfers between devices  52.1 us (10%)
  other arithmetic  44 us (9%)
    psum x1, blocking collectives, local(): lax.psum((jnp.sum(onehot * loss_part[:, None], axis=0), jnp.sum(onehot, a...  82.2 us
    all_to_all x1, blocking collectives, local(): lax.all_to_all(attended, 'seq', split_axis=1, concat_axis=2, tiled=True)  32.4 us
    unnamed x39, local copies, waits for them, and re-layouts  29.2 us
    all_to_all x1, waiting for transfers between devices, local(): lax.all_to_all(errors.astype(jnp.bfloat16), 'seq', split_axis=2, concat_a...  24.3 us
    all_to_all x1, waiting for transfers between devices, local(): lax.all_to_all(grad_query, 'seq', split_axis=1, concat_axis=2, tiled=True)  21.9 us
    all_to_all x1, waiting for transfers between devices, local(): lax.all_to_all(grad_key, 'seq', split_axis=1, concat_axis=2, tiled=True)  19.8 us
    all_to_all x1, waiting for transfers between devices, local(): lax.all_to_all(query_rot, 'seq', split_axis=2, concat_axis=1, tiled=True)  19.6 us
    reduce_sum x2, other arithmetic, softmax_parts(): row_total = jnp.sum(exp_scores, axis=-1, keepdims=True)  17.3 us
  transfers between devices with their start and end apart: 7, of which 6 were waited for; matrix products, arithmetic and copies ran while one was open for 12% of the time, Pallas kernels for 0%

commit v1 on v0

v1 whole, which is shorter than its diff:
```python
import functools
import math

import jax
import jax.numpy as jnp
import numpy as np
from jax import lax
from jax.experimental import pallas as pl
from jax.experimental.pallas import tpu as pltpu
from jax.sharding import PartitionSpec as P

MESH = pl.DeviceIdType.MESH
HD = 128
LEN = 2048
NB = 8
QUARTER = HD // 4
ZS, YS = 8, 4
QB = 256
F32 = jnp.float32
BF16 = jnp.bfloat16


def kernel(
    n_dp,
    n_seq,
    q_ref,
    k_ref,
    v_ref,
    t_ref,
    scale_ref,
    frame_ref,
    freq_ref,
    bucket_ref,
    oq_ref,
    ok_ref,
    ov_ref,
    send_in,
    recv_in,
    send_g,
    recv_g,
    grad_k,
    grad_v,
    loss_acc,
    loss_mine,
    loss_dp,
    loss_plane,
    loss_seq,
    in_send,
    in_recv,
    g_send,
    g_recv,
    dp_send,
    dp_recv,
    seq_send,
    seq_recv,
    own_sem,
):
    samples, rows, width = q_ref.shape
    dp = lax.axis_index("dp")
    me = lax.axis_index("seq")
    my_z, my_y = me // YS, me % YS

    def partner(i):
        a, dy = i // YS, i % YS
        half = (a + 1) // 2
        dz = half * (1 - 2 * (a % 2)) + ZS
        return ((my_z + dz) % ZS) * YS + (my_y + dy) % YS

    barrier = pltpu.get_barrier_semaphore()

    @pl.loop(1, n_seq)
    def _(i):
        pl.semaphore_signal(barrier, inc=1, device_id=(dp, (me + i) % n_seq), device_id_type=MESH)

    @pl.loop(1, n_dp)
    def _(i):
        pl.semaphore_signal(barrier, inc=1, device_id=((dp + i) % n_dp, me), device_id_type=MESH)

    pl.semaphore_wait(barrier, n_seq + n_dp - 2)

    lane = lax.broadcasted_iota(jnp.int32, (1, HD), 1)

    def tables(s):
        eye = lax.broadcasted_iota(jnp.int32, (rows, rows), 0) == lax.broadcasted_iota(
            jnp.int32, (rows, rows), 1
        )
        ids = frame_ref[s : s + 1, :].astype(F32)
        column = jnp.sum(jnp.where(eye, ids, 0.0), axis=1, keepdims=True)
        angle = column * freq_ref[...]
        cosine = jnp.where(lane < 2 * QUARTER, jnp.cos(angle), 1.0)
        sine = jnp.sin(angle)
        low = jnp.where(lane < QUARTER, -sine, 0.0)
        high = jnp.where((lane >= QUARTER) & (lane < 2 * QUARTER), sine, 0.0)
        return cosine, low, high

    def turn(x, cosine, low, high):
        return (
            x * cosine
            + pltpu.roll(x, HD - QUARTER, 1) * low
            + pltpu.roll(x, QUARTER, 1) * high
        )

    def in_copy(s, i):
        to = partner(i)
        return pltpu.make_async_remote_copy(
            src_ref=send_in.at[s, to],
            dst_ref=recv_in.at[s, :, pl.ds(pl.multiple_of(me * rows, rows), rows), :],
            send_sem=in_send.at[s, i],
            recv_sem=in_recv.at[s, me],
            device_id=(dp, to),
            device_id_type=MESH,
        )

    def in_own(s):
        return pltpu.make_async_copy(
            send_in.at[s, me],
            recv_in.at[s, :, pl.ds(pl.multiple_of(me * rows, rows), rows), :],
            own_sem.at[0, s],
        )

    def wait_in(s):
        @pl.loop(1, n_seq)
        def _(i):
            src = (me + i) % n_seq
            pltpu.make_async_remote_copy(
                src_ref=send_in.at[s, src],
                dst_ref=recv_in.at[s, :, pl.ds(pl.multiple_of(src * rows, rows), rows), :],
                send_sem=in_send.at[s, i],
                recv_sem=in_recv.at[s, src],
                device_id=(dp, src),
                device_id_type=MESH,
            ).wait_recv()

        in_own(s).wait()

    def g_copy(s, i):
        to = partner(i)
        return pltpu.make_async_remote_copy(
            src_ref=send_g.at[s, :, pl.ds(pl.multiple_of(to * rows, rows), rows), :],
            dst_ref=recv_g.at[s, me],
            send_sem=g_send.at[s, i],
            recv_sem=g_recv.at[s, me],
            device_id=(dp, to),
            device_id_type=MESH,
        )

    def g_own(s):
        return pltpu.make_async_copy(
            send_g.at[s, :, pl.ds(pl.multiple_of(me * rows, rows), rows), :],
            recv_g.at[s, me],
            own_sem.at[1, s],
        )

    def prepare(s):
        turns = tables(s)
        scales = scale_ref[s]
        head_lane = lax.broadcasted_iota(jnp.int32, scales.shape, 1)

        def fill(head):
            columns = pl.ds(pl.multiple_of(head * HD, HD), HD)
            send_in[s, head, 0] = turn(q_ref[s, :, columns].astype(F32), *turns).astype(BF16)
            send_in[s, head, 1] = turn(k_ref[s, :, columns].astype(F32), *turns).astype(BF16)
            scale = jnp.sum(jnp.where(head_lane == head, scales, 0.0), axis=1, keepdims=True)
            send_in[s, head, 2] = (v_ref[s, :, columns].astype(F32) * scale).astype(BF16)
            send_in[s, head, 3] = t_ref[s, :, columns]

        @pl.loop(1, n_seq)
        def _(j):
            i = n_seq - j
            fill(partner(i))
            if s > 0:
                in_copy(s - 1, i).wait_send()
            in_copy(s, i).start()

        fill(me)
        in_own(s).start()

    def attend(s):
        grad_k[...] = jnp.zeros_like(grad_k)
        grad_v[...] = jnp.zeros_like(grad_v)
        loss_acc[s] = jnp.zeros_like(loss_acc[s])

        @pl.loop(0, LEN // QB)
        def _(b):
            block = pl.ds(pl.multiple_of(b * QB, QB), QB)
            q = recv_in[s, 0, block]
            k = recv_in[s, 1]
            v = recv_in[s, 2]
            scores = lax.dot_general(q, k, (((1,), (1,)), ((), ())), preferred_element_type=F32)
            top = jnp.max(scores, axis=1, keepdims=True)
            e = jnp.exp2((scores - top) * (HD**-0.5 * math.log2(math.e)))
            p = e * (1.0 / jnp.sum(e, axis=1, keepdims=True))
            p_low = p.astype(BF16)
            attended = jnp.dot(p_low, v, preferred_element_type=F32).astype(BF16).astype(F32)
            errors = attended - recv_in[s, 3, block].astype(F32)
            loss_acc[s] += jnp.sum((errors * errors).reshape(QB // 8, 8, HD), axis=0)
            cotangent = errors.astype(BF16)
            delta = jnp.sum(cotangent.astype(F32) * attended, axis=1, keepdims=True)
            grad_v[...] += lax.dot_general(
                p_low, cotangent, (((0,), (0,)), ((), ())), preferred_element_type=F32
            )
            grad_p = lax.dot_general(
                cotangent, v, (((1,), (1,)), ((), ())), preferred_element_type=F32
            )
            grad_s = (p * (grad_p - delta) * HD**-0.5).astype(BF16)
            send_g[s, 0, block] = jnp.dot(grad_s, k, preferred_element_type=F32).astype(BF16)
            grad_k[...] += lax.dot_general(
                grad_s, q, (((0,), (0,)), ((), ())), preferred_element_type=F32
            )

        send_g[s, 1] = grad_k[...].astype(BF16)
        send_g[s, 2] = grad_v[...].astype(BF16)

    def start_g(s):
        @pl.loop(1, n_seq)
        def _(j):
            g_copy(s, n_seq - j).start()

        g_own(s).start()

    for s in range(samples):
        prepare(s)
    for s in range(samples):
        wait_in(s)
        attend(s)
        if s == 0:
            @pl.loop(1, n_seq)
            def _(i):
                in_copy(samples - 1, i).wait_send()

        if s < samples - 1:
            start_g(s)

    mine = jnp.zeros((8, HD), F32)
    for s in range(samples):
        bucket = bucket_ref[s]
        total = jnp.sum(jnp.sum(loss_acc[s], axis=0, keepdims=True), axis=1, keepdims=True)
        mine += jnp.where(lane == bucket, total / (LEN * width), 0.0)
        mine += jnp.where(lane == bucket + NB, 1.0 / n_seq, 0.0)
    loss_mine[...] = mine

    def dp_copy(i):
        to = (dp + i) % n_dp
        return pltpu.make_async_remote_copy(
            src_ref=loss_mine,
            dst_ref=loss_dp.at[dp],
            send_sem=dp_send.at[i],
            recv_sem=dp_recv.at[dp],
            device_id=(to, me),
            device_id_type=MESH,
        )

    def seq_copy(i):
        to = (me + i) % n_seq
        return pltpu.make_async_remote_copy(
            src_ref=loss_plane,
            dst_ref=loss_seq.at[me],
            send_sem=seq_send.at[i],
            recv_sem=seq_recv.at[me],
            device_id=(dp, to),
            device_id_type=MESH,
        )

    @pl.loop(1, n_dp)
    def _(i):
        dp_copy(i).start()

    loss_dp[dp] = mine

    @pl.loop(1, n_dp)
    def _(i):
        src = (dp + i) % n_dp
        pltpu.make_async_remote_copy(
            src_ref=loss_mine,
            dst_ref=loss_dp.at[src],
            send_sem=dp_send.at[i],
            recv_sem=dp_recv.at[src],
            device_id=(src, me),
            device_id_type=MESH,
        ).wait_recv()

    plane = jnp.sum(loss_dp[...], axis=0)
    loss_plane[...] = plane

    @pl.loop(1, n_seq)
    def _(i):
        seq_copy(i).start()

    loss_seq[me] = plane
    start_g(samples - 1)

    @pl.loop(1, n_seq)
    def _(i):
        src = (me + i) % n_seq
        pltpu.make_async_remote_copy(
            src_ref=loss_plane,
            dst_ref=loss_seq.at[src],
            send_sem=seq_send.at[i],
            recv_sem=seq_recv.at[src],
            device_id=(dp, src),
            device_id_type=MESH,
        ).wait_recv()

    buckets = jnp.sum(loss_seq[...], axis=0)[0:1, :]
    sum_loss = jnp.sum(jnp.where(lane < NB, buckets, 0.0), axis=1, keepdims=True)
    sum_count = jnp.sum(
        jnp.where((lane >= NB) & (lane < 2 * NB), buckets, 0.0), axis=1, keepdims=True
    )
    mean_all = sum_loss / sum_count

    for s in range(samples):
        bucket = bucket_ref[s]
        chosen_loss = jnp.sum(jnp.where(lane == bucket, buckets, 0.0), axis=1, keepdims=True)
        chosen_count = jnp.sum(
            jnp.where(lane == bucket + NB, buckets, 0.0), axis=1, keepdims=True
        )
        weight = mean_all / (chosen_loss / chosen_count + 1e-5)
        cosine, low, high = tables(s)
        scales = scale_ref[s]
        head_lane = lax.broadcasted_iota(jnp.int32, scales.shape, 1)

        def finish(head):
            columns = pl.ds(pl.multiple_of(head * HD, HD), HD)
            for array, out in ((0, oq_ref), (1, ok_ref)):
                turned = turn(recv_g[s, head, array].astype(F32), cosine, -low, -high)
                out[s, :, columns] = (weight * turned).astype(BF16)
            scale = jnp.sum(jnp.where(head_lane == head, scales, 0.0), axis=1, keepdims=True)
            ov_ref[s, :, columns] = (weight * recv_g[s, head, 2].astype(F32) * scale).astype(BF16)

        g_own(s).wait()
        finish(me)

        @pl.loop(1, n_seq)
        def _(j):
            i = n_seq - j
            src = (me + i) % n_seq
            pltpu.make_async_remote_copy(
                src_ref=send_g.at[s, :, pl.ds(pl.multiple_of(src * rows, rows), rows), :],
                dst_ref=recv_g.at[s, src],
                send_sem=g_send.at[s, i],
                recv_sem=g_recv.at[s, src],
                device_id=(dp, src),
                device_id_type=MESH,
            ).wait_recv()
            finish(src)

    @pl.loop(1, n_seq)
    def _(i):
        for s in range(samples):
            g_copy(s, i).wait_send()
        seq_copy(i).wait_send()

    @pl.loop(1, n_dp)
    def _(i):
        dp_copy(i).wait_send()


def local(n_dp, n_seq, q, k, v, scales, targets, frame_ids, bucket_ids):
    samples, rows, width = q.shape
    exponent = np.arange(HD) % QUARTER / QUARTER
    freq = np.where(np.arange(HD) < 2 * QUARTER, 10000.0 ** (-exponent), 0.0)
    freq = jnp.asarray(freq[None, :], F32)
    out = jax.ShapeDtypeStruct(q.shape, BF16)
    vmem = pl.BlockSpec(memory_space=pltpu.VMEM)
    dma = pltpu.SemaphoreType.DMA
    return tuple(
        pl.pallas_call(
            functools.partial(kernel, n_dp, n_seq),
            out_shape=(out, out, out),
            in_specs=[vmem] * 7 + [pl.BlockSpec(memory_space=pltpu.SMEM)],
            out_specs=(vmem, vmem, vmem),
            scratch_shapes=[
                pltpu.VMEM((samples, n_seq, 4, rows, HD), BF16),
                pltpu.VMEM((samples, 4, LEN, HD), BF16),
                pltpu.VMEM((samples, 3, LEN, HD), BF16),
                pltpu.VMEM((samples, n_seq, 3, rows, HD), BF16),
                pltpu.VMEM((LEN, HD), F32),
                pltpu.VMEM((LEN, HD), F32),
                pltpu.VMEM((samples, 8, HD), F32),
                pltpu.VMEM((8, HD), F32),
                pltpu.VMEM((n_dp, 8, HD), F32),
                pltpu.VMEM((8, HD), F32),
                pltpu.VMEM((n_seq, 8, HD), F32),
                dma((samples, n_seq)),
                dma((samples, n_seq)),
                dma((samples, n_seq)),
                dma((samples, n_seq)),
                dma((n_dp,)),
                dma((n_dp,)),
                dma((n_seq,)),
                dma((n_seq,)),
                dma((2, samples)),
            ],
            compiler_params=pltpu.CompilerParams(
                collective_id=0, has_side_effects=True, vmem_limit_bytes=58 << 20
            ),
        )(q, k, v, targets, scales, frame_ids, freq, bucket_ids)
    )


def solution(mesh):
    spec = P("dp", "seq", None)
    return jax.shard_map(
        functools.partial(local, mesh.shape["dp"], mesh.shape["seq"]),
        mesh=mesh,
        in_specs=(spec, spec, spec, spec, spec, P("dp", "seq"), P("dp")),
        out_specs=(spec, spec, spec),
        check_vma=False,
    )
```

time: 509 us -> 197 us (0.39); the launches traced: 500 us -> 197 us
  Pallas kernels: 0 us -> 190 us
  blocking collectives: 115 us -> 0 us
  waiting for transfers between devices: 110 us -> 0 us
  local copies, waits for them, and re-layouts: 106 us -> 6.42 us
  matrix products: 70.2 us -> 0 us
  starting transfers between devices: 52.1 us -> 0 us
  other arithmetic: 44 us -> 0 us
    pallas_call x0 -> x1, Pallas kernels: none -> 190 us  [local(): pl.pallas_call(functools.partial(kernel, n_dp, n_seq), out_shape=(out, ou...]
    all_to_all x7 -> x0, waiting for transfers between devices: 110 us -> none  [the longest x1 24.3 us: local(): lax.all_to_all(errors.astype(jnp.bfloat16), 'seq', split_axis=2, concat_a...]
    psum x1 -> x0, blocking collectives: 82.2 us -> none  [local(): lax.psum((jnp.sum(onehot * loss_part[:, None], axis=0), jnp.sum(onehot, a...]
    dot_general x14 -> x0, matrix products: 70.2 us -> none  [the longest x2 16.2 us: softmax_parts(): jnp.einsum('qhd,khd->hqk', query_rows, key_rows, preferred_element_type=j...]
    all_to_all x7 -> x0, starting transfers between devices: 52.1 us -> none  [the longest x1 12.2 us: local(): lax.all_to_all(value_deq, 'seq', split_axis=2, concat_axis=1, tiled=True)]
    all_to_all x1 -> x0, blocking collectives: 32.4 us -> none  [local(): lax.all_to_all(attended, 'seq', split_axis=1, concat_axis=2, tiled=True)]
    while x36 -> x0, local copies, waits for them, and re-layouts: 27.3 us -> none
    unnamed x39 -> x8, local copies, waits for them, and re-layouts: 29.2 us -> 6.42 us
  transfers between devices with their start and end apart: 7 -> 0, of which waited for: 6 -> 0; matrix products, arithmetic and copies ran while one was open for 12% -> 0% of each run, Pallas kernels for 0% -> 0%
where the time goes in v1:
time: 197 us
  Pallas kernels  190 us (96%)
  local copies, waits for them, and re-layouts  6.42 us (3%)
    pallas_call x1, Pallas kernels, local(): pl.pallas_call(functools.partial(kernel, n_dp, n_seq), out_shape=(out, ou...  190 us
    unnamed x8, local copies, waits for them, and re-layouts  6.42 us

profile of v1, /device:TPU:1, one launch (start us, length us, event | category | flops | bytes accessed | tf_op | source)
XLA Modules:
  0.0 196.8 jit_solution(8974325015022525090)
XLA Ops:
  0.6 1.5 copy.11.scale_ref
  2.1 189.7 %shard_map.103 = (bf16[2,64,4096]{2,1,0:T(8,128)(2,1)}, bf16[2,64,4096]{2,1,0:T(8,128)(2,1)}, bf16[2,64,4096]{2,1,0:T(8,128)(2,1)}) custom-call(bf16[2,64,4096]{2,1,0:T(8,128)(2,1)} %q_ref.1, bf16[2,64,4096]{2,1,0:T(8,128)(2,1)} %k_ref.1, bf16[2,64,4096]{2,1,0:T(8,128)(2,1)} %v_ref.1, bf16[2,64,4096]{2,1,0:T(8,128)(2,1)} %t_ref.1, ...), custom_call_target="tpu_custom_call" | custom-call | tf_op jit(solution)/shard_map/pallas_call | solution.py:367
  191.8 0.0 copy-start.1
  191.8 2.4 %copy.15 = bf16[2,64,4096]{2,1,0:T(8,128)(2,1)} copy(bf16[2,64,4096]{2,1,0:T(8,128)(2,1)} %get-tuple-element.6) | data formatting | bytes 2097152
  194.2 0.0 copy-done.1
  194.2 0.0 copy-start
  194.2 1.0 copy.16
  195.2 0.6 copy-done
  195.8 1.0 copy.17
Async XLA Ops:
  191.8 2.4 %copy-start.1 = (bf16[2,64,4096]{2,1,0:T(8,128)(2,1)S(1)}, bf16[2,64,4096]{2,1,0:T(8,128)(2,1)}, u32[]{:S(2)}) copy-start(bf16[2,64,4096]{2,1,0:T(8,128)(2,1)} %get-tuple-element.7) | copy-start | bytes 3145732
  194.2 1.6 copy-start

commit v2 on v1

--- a/solution.py
+++ b/solution.py
@@ -18,6 +18,12 @@
 QB = 256
 F32 = jnp.float32
 BF16 = jnp.bfloat16
+
+
+def turn(x, cosine, low, high):
+    return (
+        x * cosine + pltpu.roll(x, HD - QUARTER, 1) * low + pltpu.roll(x, QUARTER, 1) * high
+    )
 
 
 def kernel(
@@ -31,13 +37,13 @@
     frame_ref,
     freq_ref,
     bucket_ref,
-    oq_ref,
-    ok_ref,
-    ov_ref,
+    recv_g,
+    turn_ref,
+    weighed_ref,
+    held,
     send_in,
     recv_in,
     send_g,
-    recv_g,
     grad_k,
     grad_v,
     loss_acc,
@@ -54,8 +60,10 @@
     seq_send,
     seq_recv,
     own_sem,
+    load_sem,
 ):
     samples, rows, width = q_ref.shape
+    last = samples - 1
     dp = lax.axis_index("dp")
     me = lax.axis_index("seq")
     my_z, my_y = me // YS, me % YS
@@ -76,29 +84,29 @@
     def _(i):
         pl.semaphore_signal(barrier, inc=1, device_id=((dp + i) % n_dp, me), device_id_type=MESH)
 
-    pl.semaphore_wait(barrier, n_seq + n_dp - 2)
+    def load(s, array):
+        source = (q_ref, k_ref, v_ref, t_ref)[array]
+        return pltpu.make_async_copy(source.at[s], held.at[s, array], load_sem.at[s, array])
+
+    for s in range(samples):
+        for array in range(4):
+            load(s, array).start()
 
     lane = lax.broadcasted_iota(jnp.int32, (1, HD), 1)
 
-    def tables(s):
+    def upright(row):
         eye = lax.broadcasted_iota(jnp.int32, (rows, rows), 0) == lax.broadcasted_iota(
             jnp.int32, (rows, rows), 1
         )
-        ids = frame_ref[s : s + 1, :].astype(F32)
-        column = jnp.sum(jnp.where(eye, ids, 0.0), axis=1, keepdims=True)
-        angle = column * freq_ref[...]
+        return jnp.sum(jnp.where(eye, row, 0.0), axis=1, keepdims=True)
+
+    def tables(s):
+        angle = upright(frame_ref[s : s + 1, :].astype(F32)) * freq_ref[...]
         cosine = jnp.where(lane < 2 * QUARTER, jnp.cos(angle), 1.0)
         sine = jnp.sin(angle)
         low = jnp.where(lane < QUARTER, -sine, 0.0)
         high = jnp.where((lane >= QUARTER) & (lane < 2 * QUARTER), sine, 0.0)
         return cosine, low, high
-
-    def turn(x, cosine, low, high):
-        return (
-            x * cosine
-            + pltpu.roll(x, HD - QUARTER, 1) * low
-            + pltpu.roll(x, QUARTER, 1) * high
-        )
 
     def in_copy(s, i):
         to = partner(i)
@@ -153,27 +161,17 @@
 
     def prepare(s):
         turns = tables(s)
-        scales = scale_ref[s]
-        head_lane = lax.broadcasted_iota(jnp.int32, scales.shape, 1)
-
-        def fill(head):
+        for array in range(4):
+            load(s, array).wait()
+
+        @pl.loop(0, n_seq)
+        def _(head):
             columns = pl.ds(pl.multiple_of(head * HD, HD), HD)
-            send_in[s, head, 0] = turn(q_ref[s, :, columns].astype(F32), *turns).astype(BF16)
-            send_in[s, head, 1] = turn(k_ref[s, :, columns].astype(F32), *turns).astype(BF16)
-            scale = jnp.sum(jnp.where(head_lane == head, scales, 0.0), axis=1, keepdims=True)
-            send_in[s, head, 2] = (v_ref[s, :, columns].astype(F32) * scale).astype(BF16)
-            send_in[s, head, 3] = t_ref[s, :, columns]
-
-        @pl.loop(1, n_seq)
-        def _(j):
-            i = n_seq - j
-            fill(partner(i))
-            if s > 0:
-                in_copy(s - 1, i).wait_send()
-            in_copy(s, i).start()
-
-        fill(me)
-        in_own(s).start()
+            send_in[s, head, 0] = turn(held[s, 0, :, columns].astype(F32), *turns).astype(BF16)
+            send_in[s, head, 1] = turn(held[s, 1, :, columns].astype(F32), *turns).astype(BF16)
+            scale = upright(scale_ref[s, pl.ds(head, 1), :])
+            send_in[s, head, 2] = (held[s, 2, :, columns].astype(F32) * scale).astype(BF16)
+            send_in[s, head, 3] = held[s, 3, :, columns]
 
     def attend(s):
         grad_k[...] = jnp.zeros_like(grad_k)
@@ -211,6 +209,16 @@
         send_g[s, 1] = grad_k[...].astype(BF16)
         send_g[s, 2] = grad_v[...].astype(BF16)
 
+    def start_in(s):
+        @pl.loop(1, n_seq)
+        def _(j):
+            i = n_seq - j
+            if s > 0:
+                in_copy(s - 1, i).wait_send()
+            in_copy(s, i).start()
+
+        in_own(s).start()
+
     def start_g(s):
         @pl.loop(1, n_seq)
         def _(j):
@@ -218,18 +226,25 @@
 
         g_own(s).start()
 
-    for s in range(samples):
+    prepare(0)
+    pl.semaphore_wait(barrier, n_seq + n_dp - 2)
+    start_in(0)
+    for s in range(1, samples):
         prepare(s)
-    for s in range(samples):
+        start_in(s)
+
+    @pl.loop(0, samples)
+    def _(s):
         wait_in(s)
         attend(s)
-        if s == 0:
+
+        @pl.when(s == 0)
+        def _():
             @pl.loop(1, n_seq)
             def _(i):
-                in_copy(samples - 1, i).wait_send()
-
-        if s < samples - 1:
-            start_g(s)
+                in_copy(last, i).wait_send()
+
+        start_g(s)
 
     mine = jnp.zeros((8, HD), F32)
     for s in range(samples):
@@ -287,7 +302,6 @@
         seq_copy(i).start()
 
     loss_seq[me] = plane
-    start_g(samples - 1)
 
     @pl.loop(1, n_seq)
     def _(i):
@@ -316,23 +330,16 @@
         )
         weight = mean_all / (chosen_loss / chosen_count + 1e-5)
         cosine, low, high = tables(s)
-        scales = scale_ref[s]
-        head_lane = lax.broadcasted_iota(jnp.int32, scales.shape, 1)
-
-        def finish(head):
-            columns = pl.ds(pl.multiple_of(head * HD, HD), HD)
-            for array, out in ((0, oq_ref), (1, ok_ref)):
-                turned = turn(recv_g[s, head, array].astype(F32), cosine, -low, -high)
-                out[s, :, columns] = (weight * turned).astype(BF16)
-            scale = jnp.sum(jnp.where(head_lane == head, scales, 0.0), axis=1, keepdims=True)
-            ov_ref[s, :, columns] = (weight * recv_g[s, head, 2].astype(F32) * scale).astype(BF16)
-
+        turn_ref[s, 0] = weight * cosine
+        turn_ref[s, 1] = -weight * low
+        turn_ref[s, 2] = -weight * high
+        weighed_ref[s] = weight * scale_ref[s]
+
+    for s in range(samples):
         g_own(s).wait()
-        finish(me)
 
         @pl.loop(1, n_seq)
-        def _(j):
-            i = n_seq - j
+        def _(i):
             src = (me + i) % n_seq
             pltpu.make_async_remote_copy(
                 src_ref=send_g.at[s, :, pl.ds(pl.multiple_of(src * rows, rows), rows), :],
@@ -342,7 +349,6 @@
                 device_id=(dp, src),
                 device_id_type=MESH,
             ).wait_recv()
-            finish(src)
 
     @pl.loop(1, n_seq)
     def _(i):
@@ -353,6 +359,22 @@
     @pl.loop(1, n_dp)
     def _(i):
         dp_copy(i).wait_send()
+
+
+def finish(heads, grad_ref, turn_ref, weighed_ref, oq_ref, ok_ref, ov_ref):
+    rows = grad_ref.shape[3]
+    cosine, low, high = turn_ref[0, 0], turn_ref[0, 1], turn_ref[0, 2]
+    eye = lax.broadcasted_iota(jnp.int32, (rows, rows), 0) == lax.broadcasted_iota(
+        jnp.int32, (rows, rows), 1
+    )
+    first = pl.program_id(1) * heads
+    for h in range(heads):
+        columns = slice(h * HD, (h + 1) * HD)
+        oq_ref[0, :, columns] = turn(grad_ref[0, h, 0].astype(F32), cosine, low, high).astype(BF16)
+        ok_ref[0, :, columns] = turn(grad_ref[0, h, 1].astype(F32), cosine, low, high).astype(BF16)
+        row = weighed_ref[0, pl.ds(first + h, 1), :]
+        scale = jnp.sum(jnp.where(eye, row, 0.0), axis=1, keepdims=True)
+        ov_ref[0, :, columns] = (grad_ref[0, h, 2].astype(F32) * scale).astype(BF16)
 
 
 def local(n_dp, n_seq, q, k, v, scales, targets, frame_ids, bucket_ids):
@@ -360,41 +382,63 @@
     exponent = np.arange(HD) % QUARTER / QUARTER
     freq = np.where(np.arange(HD) < 2 * QUARTER, 10000.0 ** (-exponent), 0.0)
     freq = jnp.asarray(freq[None, :], F32)
+    scales = jnp.swapaxes(scales, 1, 2)
+    vmem = pl.BlockSpec(memory_space=pltpu.VMEM)
+    smem = pl.BlockSpec(memory_space=pltpu.SMEM)
+    anywhere = pl.BlockSpec(memory_space=pl.ANY)
+    dma = pltpu.SemaphoreType.DMA
+    grads, turns, weighed = pl.pallas_call(
+        functools.partial(kernel, n_dp, n_seq),
+        out_shape=(
+            jax.ShapeDtypeStruct((samples, n_seq, 3, rows, HD), BF16),
+            jax.ShapeDtypeStruct((samples, 3, rows, HD), F32),
+            jax.ShapeDtypeStruct(scales.shape, F32),
+        ),
+        in_specs=[anywhere] * 4 + [vmem] * 3 + [smem],
+        out_specs=(anywhere, vmem, vmem),
+        scratch_shapes=[
+            pltpu.VMEM((samples, 4, rows, width), BF16),
+            pltpu.VMEM((samples, n_seq, 4, rows, HD), BF16),
+            pltpu.VMEM((samples, 4, LEN, HD), BF16),
+            pltpu.VMEM((samples, 3, LEN, HD), BF16),
+            pltpu.VMEM((LEN, HD), F32),
+            pltpu.VMEM((LEN, HD), F32),
+            pltpu.VMEM((samples, 8, HD), F32),
+            pltpu.VMEM((8, HD), F32),
+            pltpu.VMEM((n_dp, 8, HD), F32),
+            pltpu.VMEM((8, HD), F32),
+            pltpu.VMEM((n_seq, 8, HD), F32),
+            dma((samples, n_seq)),
+            dma((samples, n_seq)),
+            dma((samples, n_seq)),
+            dma((samples, n_seq)),
+            dma((n_dp,)),
+            dma((n_dp,)),
+            dma((n_seq,)),
+            dma((n_seq,)),
+            dma((2, samples)),
+            dma((samples, 4)),
+        ],
+        compiler_params=pltpu.CompilerParams(
+            collective_id=0, has_side_effects=True, vmem_limit_bytes=58 << 20
+        ),
+    )(q, k, v, targets, scales, frame_ids, freq, bucket_ids)
+    heads = 8
     out = jax.ShapeDtypeStruct(q.shape, BF16)
-    vmem = pl.BlockSpec(memory_space=pltpu.VMEM)
-    dma = pltpu.SemaphoreType.DMA
+    out_spec = pl.BlockSpec((1, rows, heads * HD), lambda s, g: (s, 0, g))
     return tuple(
         pl.pallas_call(
-            functools.partial(kernel, n_dp, n_seq),
+            functools.partial(finish, heads),
+            grid=(samples, n_seq // heads),
             out_shape=(out, out, out),
-            in_specs=[vmem] * 7 + [pl.BlockSpec(memory_space=pltpu.SMEM)],
-            out_specs=(vmem, vmem, vmem),
-            scratch_shapes=[
-                pltpu.VMEM((samples, n_seq, 4, rows, HD), BF16),
-                pltpu.VMEM((samples, 4, LEN, HD), BF16),
-                pltpu.VMEM((samples, 3, LEN, HD), BF16),
-                pltpu.VMEM((samples, n_seq, 3, rows, HD), BF16),
-                pltpu.VMEM((LEN, HD), F32),
-                pltpu.VMEM((LEN, HD), F32),
-                pltpu.VMEM((samples, 8, HD), F32),
-                pltpu.VMEM((8, HD), F32),
-                pltpu.VMEM((n_dp, 8, HD), F32),
-                pltpu.VMEM((8, HD), F32),
-                pltpu.VMEM((n_seq, 8, HD), F32),
-                dma((samples, n_seq)),
-                dma((samples, n_seq)),
-                dma((samples, n_seq)),
-                dma((samples, n_seq)),
-                dma((n_dp,)),
-                dma((n_dp,)),
-                dma((n_seq,)),
-                dma((n_seq,)),
-                dma((2, samples)),
+            in_specs=[
+                pl.BlockSpec((1, heads, 3, rows, HD), lambda s, g: (s, g, 0, 0, 0)),
+                pl.BlockSpec((1, 3, rows, HD), lambda s, g: (s, 0, 0, 0)),
+                pl.BlockSpec((1, n_seq, rows), lambda s, g: (s, 0, 0)),
             ],
-            compiler_params=pltpu.CompilerParams(
-                collective_id=0, has_side_effects=True, vmem_limit_bytes=58 << 20
-            ),
-        )(q, k, v, targets, scales, frame_ids, freq, bucket_ids)
+            out_specs=(out_spec, out_spec, out_spec),
+            compiler_params=pltpu.CompilerParams(vmem_limit_bytes=58 << 20),
+        )(grads, turns, weighed)
     )
 
 

time: 197 us -> 201 us (1.020)
  Pallas kernels: 190 us -> 200 us
  local copies, waits for them, and re-layouts: 6.42 us -> 0 us
    pallas_call x1 -> x2, Pallas kernels: 190 us -> 200 us  [the longest x1 192 us: local(): pl.pallas_call(functools.partial(kernel, n_dp, n_seq), out_shape=(jax.Sha...]
    unnamed x8 -> x0, local copies, waits for them, and re-layouts: 6.42 us -> none
where the time goes in v2:
time: 201 us; the launch traced here: 200 us
  Pallas kernels  200 us (100%)
    pallas_call x1, Pallas kernels, local(): pl.pallas_call(functools.partial(kernel, n_dp, n_seq), out_shape=(jax.Sha...  192 us
    pallas_call x1, Pallas kernels, local(): pl.pallas_call(functools.partial(finish, heads), grid=(samples, n_seq //...  7.84 us

profile of v2, /device:TPU:1, one launch (start us, length us, event | category | flops | bytes accessed | tf_op | source)
XLA Modules:
  0.0 200.4 jit_solution(6125518322682888090)
XLA Ops:
  0.6 192.0 %shard_map.103 = (bf16[2,32,3,64,128]{4,3,2,1,0:T(8,128)(2,1)}, f32[2,3,64,128]{3,2,1,0:T(8,128)}, f32[2,32,64]{2,1,0:T(8,128)}) custom-call(bf16[2,64,4096]{2,1,0:T(8,128)(2,1)} %q_ref.1, bf16[2,64,4096]{2,1,0:T(8,128)(2,1)} %k_ref.1, bf16[2,64,4096]{2,1,0:T(8,128)(2,1)} %v_ref.1, bf16[2,64,4096]{2,1,0:T(8,128)(2,1)} %t_ref.1, f32[2,32,64]{2,1,0:T(8,128)} %bitcast.1, ...), custom_call_target="tpu_custom_call" | custom-call | tf_op jit(solution)/shard_map/pallas_call | solution.py:390
  192.6 7.8 %shard_map.104 = (bf16[2,64,4096]{2,1,0:T(8,128)(2,1)}, bf16[2,64,4096]{2,1,0:T(8,128)(2,1)}, bf16[2,64,4096]{2,1,0:T(8,128)(2,1)}) custom-call(bf16[2,32,3,64,128]{4,3,2,1,0:T(8,128)(2,1)} %get-tuple-element.6.grad_ref, f32[2,3,64,128]{3,2,1,0:T(8,128)} %get-tuple-element.7.turn_ref, f32[2,32,64]{2,1,0:T(8,128)} %get-tuple-element.8.weighed_ref), custom_call_target="tpu_custom_call" | custom-call | tf_op jit(solution)/shard_map/pallas_call | solution.py:430

commit v3 on v2

--- a/solution.py
+++ b/solution.py
@@ -20,10 +20,20 @@
 BF16 = jnp.bfloat16
 
 
-def turn(x, cosine, low, high):
-    return (
-        x * cosine + pltpu.roll(x, HD - QUARTER, 1) * low + pltpu.roll(x, QUARTER, 1) * high
-    )
+def swap_matrix():
+    i = lax.broadcasted_iota(jnp.int32, (HD, HD), 0)
+    j = lax.broadcasted_iota(jnp.int32, (HD, HD), 1)
+    first = (j < QUARTER) & (i == j + QUARTER)
+    second = (j >= QUARTER) & (j < 2 * QUARTER) & (i == j - QUARTER)
+    return jnp.where(first | second, 1.0, 0.0).astype(BF16)
+
+
+def turn(blocks, cosine, sine):
+    x = jnp.concatenate(blocks, axis=0)
+    swapped = jnp.dot(x, swap_matrix(), preferred_element_type=F32)
+    shape = (len(blocks),) + blocks[0].shape
+    turned = x.astype(F32).reshape(shape) * cosine + swapped.reshape(shape) * sine
+    return turned.astype(BF16)
 
 
 def kernel(
@@ -33,14 +43,22 @@
     k_ref,
     v_ref,
     t_ref,
+    scale_hbm,
+    frame_hbm,
+    freq_hbm,
+    bucket_ref,
+    recv_g,
+    turn_hbm,
+    weighed_hbm,
     scale_ref,
     frame_ref,
     freq_ref,
-    bucket_ref,
-    recv_g,
     turn_ref,
     weighed_ref,
     held,
+    tables,
+    upright,
+    planes,
     send_in,
     recv_in,
     send_g,
@@ -53,6 +71,8 @@
     loss_seq,
     in_send,
     in_recv,
+    t_send,
+    t_recv,
     g_send,
     g_recv,
     dp_send,
@@ -61,6 +81,7 @@
     seq_recv,
     own_sem,
     load_sem,
+    side_sem,
 ):
     samples, rows, width = q_ref.shape
     last = samples - 1
@@ -84,62 +105,86 @@
     def _(i):
         pl.semaphore_signal(barrier, inc=1, device_id=((dp + i) % n_dp, me), device_id_type=MESH)
 
+    side = [
+        pltpu.make_async_copy(source, there, side_sem.at[i])
+        for i, (source, there) in enumerate(
+            ((scale_hbm, scale_ref), (frame_hbm, frame_ref), (freq_hbm, freq_ref))
+        )
+    ]
+
     def load(s, array):
-        source = (q_ref, k_ref, v_ref, t_ref)[array]
+        source = (q_ref, k_ref, v_ref)[array]
         return pltpu.make_async_copy(source.at[s], held.at[s, array], load_sem.at[s, array])
 
+    for copy in side:
+        copy.start()
     for s in range(samples):
-        for array in range(4):
+        for array in range(3):
             load(s, array).start()
 
     lane = lax.broadcasted_iota(jnp.int32, (1, HD), 1)
-
-    def upright(row):
-        eye = lax.broadcasted_iota(jnp.int32, (rows, rows), 0) == lax.broadcasted_iota(
-            jnp.int32, (rows, rows), 1
-        )
-        return jnp.sum(jnp.where(eye, row, 0.0), axis=1, keepdims=True)
-
-    def tables(s):
-        angle = upright(frame_ref[s : s + 1, :].astype(F32)) * freq_ref[...]
-        cosine = jnp.where(lane < 2 * QUARTER, jnp.cos(angle), 1.0)
+    eye = lax.broadcasted_iota(jnp.int32, (rows, rows), 0) == lax.broadcasted_iota(
+        jnp.int32, (rows, rows), 1
+    )
+
+    def ready_tables(s):
+        ids = frame_ref[s : s + 1, :].astype(F32)
+        angle = jnp.sum(jnp.where(eye, ids, 0.0), axis=1, keepdims=True) * freq_ref[...]
+        tables[s, 0] = jnp.where(lane < 2 * QUARTER, jnp.cos(angle), 1.0)
         sine = jnp.sin(angle)
-        low = jnp.where(lane < QUARTER, -sine, 0.0)
-        high = jnp.where((lane >= QUARTER) & (lane < 2 * QUARTER), sine, 0.0)
-        return cosine, low, high
-
-    def in_copy(s, i):
-        to = partner(i)
+        tables[s, 1] = jnp.where(
+            lane < QUARTER, -sine, jnp.where(lane < 2 * QUARTER, sine, 0.0)
+        )
+        columns = jnp.transpose(scale_ref[s])
+        upright[s] = columns
+        for z in range(ZS):
+            planes[s, z] = columns[:, z * YS : (z + 1) * YS]
+
+    def rows_of(device):
+        return pl.ds(pl.multiple_of(device * rows, rows), rows)
+
+    def head_of(device):
+        return pl.ds(pl.multiple_of(device * HD, HD), HD)
+
+    def in_copy(s, to, source):
         return pltpu.make_async_remote_copy(
             src_ref=send_in.at[s, to],
-            dst_ref=recv_in.at[s, :, pl.ds(pl.multiple_of(me * rows, rows), rows), :],
-            send_sem=in_send.at[s, i],
-            recv_sem=in_recv.at[s, me],
+            dst_ref=recv_in.at[s, pl.ds(0, 3), rows_of(source), :],
+            send_sem=in_send.at[s, to],
+            recv_sem=in_recv.at[s, source],
             device_id=(dp, to),
             device_id_type=MESH,
         )
 
+    def t_copy(s, to, source):
+        return pltpu.make_async_remote_copy(
+            src_ref=t_ref.at[s, :, head_of(to)],
+            dst_ref=recv_in.at[s, 3, rows_of(source), :],
+            send_sem=t_send.at[s, to],
+            recv_sem=t_recv.at[s, source],
+            device_id=(dp, to),
+            device_id_type=MESH,
+        )
+
     def in_own(s):
         return pltpu.make_async_copy(
-            send_in.at[s, me],
-            recv_in.at[s, :, pl.ds(pl.multiple_of(me * rows, rows), rows), :],
-            own_sem.at[0, s],
+            send_in.at[s, me], recv_in.at[s, pl.ds(0, 3), rows_of(me), :], own_sem.at[0, s]
+        )
+
+    def t_own(s):
+        return pltpu.make_async_copy(
+            t_ref.at[s, :, head_of(me)], recv_in.at[s, 3, rows_of(me), :], own_sem.at[2, s]
         )
 
     def wait_in(s):
         @pl.loop(1, n_seq)
         def _(i):
-            src = (me + i) % n_seq
-            pltpu.make_async_remote_copy(
-                src_ref=send_in.at[s, src],
-                dst_ref=recv_in.at[s, :, pl.ds(pl.multiple_of(src * rows, rows), rows), :],
-                send_sem=in_send.at[s, i],
-                recv_sem=in_recv.at[s, src],
-                device_id=(dp, src),
-                device_id_type=MESH,
-            ).wait_recv()
+            source = (me + i) % n_seq
+            t_copy(s, source, source).wait_recv()
+            in_copy(s, source, source).wait_recv()
 
         in_own(s).wait()
+        t_own(s).wait()
 
     def g_copy(s, i):
         to = partner(i)
@@ -159,19 +204,34 @@
             own_sem.at[1, s],
         )
 
-    def prepare(s):
-        turns = tables(s)
-        for array in range(4):
-            load(s, array).wait()
-
-        @pl.loop(0, n_seq)
-        def _(head):
-            columns = pl.ds(pl.multiple_of(head * HD, HD), HD)
-            send_in[s, head, 0] = turn(held[s, 0, :, columns].astype(F32), *turns).astype(BF16)
-            send_in[s, head, 1] = turn(held[s, 1, :, columns].astype(F32), *turns).astype(BF16)
-            scale = upright(scale_ref[s, pl.ds(head, 1), :])
-            send_in[s, head, 2] = (held[s, 2, :, columns].astype(F32) * scale).astype(BF16)
-            send_in[s, head, 3] = held[s, 3, :, columns]
+    def plane(a):
+        half = (ZS - a) // 2
+        return (my_z + half * (1 - 2 * ((ZS - 1 - a) % 2)) + ZS) % ZS
+
+    def prepare(s, z):
+        def block(array, y):
+            return held[s, array, :, pl.ds(pl.multiple_of((z * YS + y) * HD, HD), HD)]
+
+        turned = turn(
+            [block(array, y) for array in range(2) for y in range(YS)], tables[s, 0], tables[s, 1]
+        )
+        scales = planes[s, z]
+        for y in range(YS):
+            head = z * YS + y
+            send_in[s, head, 0] = turned[y]
+            send_in[s, head, 1] = turned[YS + y]
+            send_in[s, head, 2] = (block(2, y).astype(F32) * scales[:, y : y + 1]).astype(BF16)
+
+    def send(s, z):
+        for y in range(YS):
+            to = z * YS + y
+
+            @pl.when(to != me)
+            def _():
+                if s > 0:
+                    in_copy(s - 1, to, me).wait_send()
+                    t_copy(s, to, me).start()
+                in_copy(s, to, me).start()
 
     def attend(s):
         grad_k[...] = jnp.zeros_like(grad_k)
@@ -209,42 +269,46 @@
         send_g[s, 1] = grad_k[...].astype(BF16)
         send_g[s, 2] = grad_v[...].astype(BF16)
 
-    def start_in(s):
-        @pl.loop(1, n_seq)
-        def _(j):
-            i = n_seq - j
-            if s > 0:
-                in_copy(s - 1, i).wait_send()
-            in_copy(s, i).start()
-
-        in_own(s).start()
-
-    def start_g(s):
-        @pl.loop(1, n_seq)
+    def start_g(s, begin, end):
+        @pl.loop(begin, end)
         def _(j):
             g_copy(s, n_seq - j).start()
 
-        g_own(s).start()
-
-    prepare(0)
     pl.semaphore_wait(barrier, n_seq + n_dp - 2)
-    start_in(0)
-    for s in range(1, samples):
-        prepare(s)
-        start_in(s)
+
+    @pl.loop(1, n_seq)
+    def _(j):
+        t_copy(0, partner(n_seq - j), me).start()
+
+    for copy in side:
+        copy.wait()
+    for s in range(samples):
+        ready_tables(s)
+        t_own(s).start()
+    for s in range(samples):
+        for array in range(3):
+            load(s, array).wait()
+
+        @pl.loop(0, ZS)
+        def _(a):
+            prepare(s, plane(a))
+            send(s, plane(a))
+
+        in_own(s).start()
 
     @pl.loop(0, samples)
     def _(s):
         wait_in(s)
         attend(s)
 
-        @pl.when(s == 0)
+        @pl.when(s < last)
         def _():
             @pl.loop(1, n_seq)
             def _(i):
-                in_copy(last, i).wait_send()
-
-        start_g(s)
+                in_copy(last, (me + i) % n_seq, me).wait_send()
+
+            start_g(s, 1, n_seq)
+            g_own(s).start()
 
     mine = jnp.zeros((8, HD), F32)
     for s in range(samples):
@@ -281,6 +345,8 @@
         dp_copy(i).start()
 
     loss_dp[dp] = mine
+    start_g(last, 1, 2 * n_seq // 3)
+    g_own(last).start()
 
     @pl.loop(1, n_dp)
     def _(i):
@@ -294,14 +360,15 @@
             device_id_type=MESH,
         ).wait_recv()
 
-    plane = jnp.sum(loss_dp[...], axis=0)
-    loss_plane[...] = plane
+    plane_loss = jnp.sum(loss_dp[...], axis=0)
+    loss_plane[...] = plane_loss
 
     @pl.loop(1, n_seq)
     def _(i):
         seq_copy(i).start()
 
-    loss_seq[me] = plane
+    loss_seq[me] = plane_loss
+    start_g(last, 2 * n_seq // 3, n_seq)
 
     @pl.loop(1, n_seq)
     def _(i):
@@ -329,11 +396,16 @@
             jnp.where(lane == bucket + NB, buckets, 0.0), axis=1, keepdims=True
         )
         weight = mean_all / (chosen_loss / chosen_count + 1e-5)
-        cosine, low, high = tables(s)
-        turn_ref[s, 0] = weight * cosine
-        turn_ref[s, 1] = -weight * low
-        turn_ref[s, 2] = -weight * high
-        weighed_ref[s] = weight * scale_ref[s]
+        turn_ref[s, 0] = weight * tables[s, 0]
+        turn_ref[s, 1] = -weight * tables[s, 1]
+        weighed_ref[s] = weight * upright[s]
+
+    results = (
+        pltpu.make_async_copy(turn_ref, turn_hbm, side_sem.at[0]),
+        pltpu.make_async_copy(weighed_ref, weighed_hbm, side_sem.at[1]),
+    )
+    for copy in results:
+        copy.start()
 
     for s in range(samples):
         g_own(s).wait()
@@ -354,27 +426,96 @@
     def _(i):
         for s in range(samples):
             g_copy(s, i).wait_send()
+            t_copy(s, (me + i) % n_seq, me).wait_send()
         seq_copy(i).wait_send()
 
     @pl.loop(1, n_dp)
     def _(i):
         dp_copy(i).wait_send()
 
-
-def finish(heads, grad_ref, turn_ref, weighed_ref, oq_ref, ok_ref, ov_ref):
-    rows = grad_ref.shape[3]
-    cosine, low, high = turn_ref[0, 0], turn_ref[0, 1], turn_ref[0, 2]
-    eye = lax.broadcasted_iota(jnp.int32, (rows, rows), 0) == lax.broadcasted_iota(
-        jnp.int32, (rows, rows), 1
+    for copy in results:
+        copy.wait()
+
+
+def finish(
+    grad_hbm,
+    turn_hbm,
+    weighed_hbm,
+    oq_hbm,
+    ok_hbm,
+    ov_hbm,
+    grad_ref,
+    turn_ref,
+    weighed_ref,
+    out_ref,
+    grad_sem,
+    side_sem,
+    out_sem,
+):
+    samples, heads, _, rows, _ = grad_ref.shape
+    part = 16
+    pieces = 4
+    each = heads // pieces
+
+    def load(s, p):
+        some = pl.ds(p * each, each)
+        return pltpu.make_async_copy(
+            grad_hbm.at[s, some], grad_ref.at[s, some], grad_sem.at[s, p]
+        )
+
+    side = (
+        pltpu.make_async_copy(turn_hbm, turn_ref, side_sem.at[0]),
+        pltpu.make_async_copy(weighed_hbm, weighed_ref, side_sem.at[1]),
     )
-    first = pl.program_id(1) * heads
-    for h in range(heads):
-        columns = slice(h * HD, (h + 1) * HD)
-        oq_ref[0, :, columns] = turn(grad_ref[0, h, 0].astype(F32), cosine, low, high).astype(BF16)
-        ok_ref[0, :, columns] = turn(grad_ref[0, h, 1].astype(F32), cosine, low, high).astype(BF16)
-        row = weighed_ref[0, pl.ds(first + h, 1), :]
-        scale = jnp.sum(jnp.where(eye, row, 0.0), axis=1, keepdims=True)
-        ov_ref[0, :, columns] = (grad_ref[0, h, 2].astype(F32) * scale).astype(BF16)
+
+    def store(s, r, array):
+        some = pl.ds(pl.multiple_of(r * part, part), part)
+        return pltpu.make_async_copy(
+            out_ref.at[array, s, some],
+            (oq_hbm, ok_hbm, ov_hbm)[array].at[s, some],
+            out_sem.at[array, s, r],
+        )
+
+    for p in range(pieces):
+        load(0, p).start()
+    for copy in side:
+        copy.start()
+    for s in range(1, samples):
+        for p in range(pieces):
+            load(s, p).start()
+    for copy in side:
+        copy.wait()
+
+    @pl.loop(0, samples)
+    def _(s):
+        for p in range(pieces):
+            load(s, p).wait()
+
+        @pl.loop(0, rows // part)
+        def _(r):
+            some = pl.ds(pl.multiple_of(r * part, part), part)
+            for array in range(2):
+                turned = turn(
+                    [grad_ref[s, h, array, some] for h in range(heads)],
+                    turn_ref[s, 0, some],
+                    turn_ref[s, 1, some],
+                )
+                for h in range(heads):
+                    out_ref[array, s, some, h * HD : (h + 1) * HD] = turned[h]
+                store(s, r, array).start()
+            scales = weighed_ref[s, some]
+            for h in range(heads):
+                out_ref[2, s, some, h * HD : (h + 1) * HD] = (
+                    grad_ref[s, h, 2, some].astype(F32) * scales[:, h : h + 1]
+                ).astype(BF16)
+            store(s, r, 2).start()
+
+    @pl.loop(0, samples)
+    def _(s):
+        @pl.loop(0, rows // part)
+        def _(r):
+            for array in range(3):
+                store(s, r, array).wait()
 
 
 def local(n_dp, n_seq, q, k, v, scales, targets, frame_ids, bucket_ids):
@@ -383,7 +524,6 @@
     freq = np.where(np.arange(HD) < 2 * QUARTER, 10000.0 ** (-exponent), 0.0)
     freq = jnp.asarray(freq[None, :], F32)
     scales = jnp.swapaxes(scales, 1, 2)
-    vmem = pl.BlockSpec(memory_space=pltpu.VMEM)
     smem = pl.BlockSpec(memory_space=pltpu.SMEM)
     anywhere = pl.BlockSpec(memory_space=pl.ANY)
     dma = pltpu.SemaphoreType.DMA
@@ -391,14 +531,22 @@
         functools.partial(kernel, n_dp, n_seq),
         out_shape=(
             jax.ShapeDtypeStruct((samples, n_seq, 3, rows, HD), BF16),
-            jax.ShapeDtypeStruct((samples, 3, rows, HD), F32),
-            jax.ShapeDtypeStruct(scales.shape, F32),
+            jax.ShapeDtypeStruct((samples, 2, rows, HD), F32),
+            jax.ShapeDtypeStruct((samples, rows, n_seq), F32),
         ),
-        in_specs=[anywhere] * 4 + [vmem] * 3 + [smem],
-        out_specs=(anywhere, vmem, vmem),
+        in_specs=[anywhere] * 7 + [smem],
+        out_specs=(anywhere, anywhere, anywhere),
         scratch_shapes=[
-            pltpu.VMEM((samples, 4, rows, width), BF16),
-            pltpu.VMEM((samples, n_seq, 4, rows, HD), BF16),
+            pltpu.VMEM(scales.shape, F32),
+            pltpu.VMEM(frame_ids.shape, jnp.int32),
+            pltpu.VMEM(freq.shape, F32),
+            pltpu.VMEM((samples, 2, rows, HD), F32),
+            pltpu.VMEM((samples, rows, n_seq), F32),
+            pltpu.VMEM((samples, 3, rows, width), BF16),
+            pltpu.VMEM((samples, 2, rows, HD), F32),
+            pltpu.VMEM((samples, rows, n_seq), F32),
+            pltpu.VMEM((samples, ZS, rows, YS), F32),
+            pltpu.VMEM((samples, n_seq, 3, rows, HD), BF16),
             pltpu.VMEM((samples, 4, LEN, HD), BF16),
             pltpu.VMEM((samples, 3, LEN, HD), BF16),
             pltpu.VMEM((LEN, HD), F32),
@@ -412,31 +560,36 @@
             dma((samples, n_seq)),
             dma((samples, n_seq)),
             dma((samples, n_seq)),
+            dma((samples, n_seq)),
+            dma((samples, n_seq)),
             dma((n_dp,)),
             dma((n_dp,)),
             dma((n_seq,)),
             dma((n_seq,)),
-            dma((2, samples)),
-            dma((samples, 4)),
+            dma((3, samples)),
+            dma((samples, 3)),
+            dma((3,)),
         ],
         compiler_params=pltpu.CompilerParams(
             collective_id=0, has_side_effects=True, vmem_limit_bytes=58 << 20
         ),
     )(q, k, v, targets, scales, frame_ids, freq, bucket_ids)
-    heads = 8
     out = jax.ShapeDtypeStruct(q.shape, BF16)
-    out_spec = pl.BlockSpec((1, rows, heads * HD), lambda s, g: (s, 0, g))
     return tuple(
         pl.pallas_call(
-            functools.partial(finish, heads),
-            grid=(samples, n_seq // heads),
+            finish,
             out_shape=(out, out, out),
-            in_specs=[
-                pl.BlockSpec((1, heads, 3, rows, HD), lambda s, g: (s, g, 0, 0, 0)),
-                pl.BlockSpec((1, 3, rows, HD), lambda s, g: (s, 0, 0, 0)),
-                pl.BlockSpec((1, n_seq, rows), lambda s, g: (s, 0, 0)),
+            in_specs=[anywhere] * 3,
+            out_specs=(anywhere,) * 3,
+            scratch_shapes=[
+                pltpu.VMEM(grads.shape, BF16),
+                pltpu.VMEM(turns.shape, F32),
+                pltpu.VMEM(weighed.shape, F32),
+                pltpu.VMEM((3,) + q.shape, BF16),
+                dma((samples, 4)),
+                dma((2,)),
+                dma((3, samples, 4)),
             ],
-            out_specs=(out_spec, out_spec, out_spec),
             compiler_params=pltpu.CompilerParams(vmem_limit_bytes=58 << 20),
         )(grads, turns, weighed)
     )

time: 201 us -> 189 us (0.940)
  Pallas kernels: 200 us -> 188 us
    pallas_call x1, Pallas kernels: 192 us -> 183 us  [local(): pl.pallas_call(functools.partial(kernel, n_dp, n_seq), out_shape=(jax.Sha...]
    pallas_call x1, Pallas kernels: 7.84 us -> 4.82 us  [local(): pl.pallas_call(finish, out_shape=(out, out, out), in_specs=[anywhere] * 3...]
where the time goes in v3:
time: 189 us
  Pallas kernels  188 us (99%)
    pallas_call x1, Pallas kernels, local(): pl.pallas_call(functools.partial(kernel, n_dp, n_seq), out_shape=(jax.Sha...  183 us
    pallas_call x1, Pallas kernels, local(): pl.pallas_call(finish, out_shape=(out, out, out), in_specs=[anywhere] * 3...  4.82 us

profile of v3, /device:TPU:1, one launch (start us, length us, event | category | flops | bytes accessed | tf_op | source)
XLA Modules:
  0.0 188.5 jit_solution(4094204474625158020)
XLA Ops:
  0.6 183.1 %shard_map.103 = (bf16[2,32,3,64,128]{4,3,2,1,0:T(8,128)(2,1)}, f32[2,2,64,128]{3,2,1,0:T(8,128)}, f32[2,64,32]{2,1,0:T(8,128)}) custom-call(bf16[2,64,4096]{2,1,0:T(8,128)(2,1)} %q_ref.1, bf16[2,64,4096]{2,1,0:T(8,128)(2,1)} %k_ref.1, bf16[2,64,4096]{2,1,0:T(8,128)(2,1)} %v_ref.1, bf16[2,64,4096]{2,1,0:T(8,128)(2,1)} %t_ref.1, f32[2,32,64]{2,1,0:T(8,128)} %bitcast.1, ...), custom_call_target="tpu_custom_call" | custom-call | tf_op jit(solution)/shard_map/pallas_call | solution.py:530
  183.7 4.8 %shard_map.104 = (bf16[2,64,4096]{2,1,0:T(8,128)(2,1)}, bf16[2,64,4096]{2,1,0:T(8,128)(2,1)}, bf16[2,64,4096]{2,1,0:T(8,128)(2,1)}) custom-call(bf16[2,32,3,64,128]{4,3,2,1,0:T(8,128)(2,1)} %get-tuple-element.6.grad_hbm, f32[2,2,64,128]{3,2,1,0:T(8,128)} %get-tuple-element.7.turn_hbm, f32[2,64,32]{2,1,0:T(8,128)} %get-tuple-element.8.weighed_hbm), custom_call_target="tpu_custom_call" | custom-call | tf_op jit(solution)/shard_map/pallas_call | solution.py:579

commit v4 on v3

--- a/solution.py
+++ b/solution.py
@@ -16,6 +16,8 @@
 QUARTER = HD // 4
 ZS, YS = 8, 4
 QB = 256
+GROUP = 8
+AHEAD = 8
 F32 = jnp.float32
 BF16 = jnp.bfloat16
 
@@ -303,14 +305,20 @@
 
         @pl.when(s < last)
         def _():
-            @pl.loop(1, n_seq)
-            def _(i):
-                in_copy(last, (me + i) % n_seq, me).wait_send()
-
-            start_g(s, 1, n_seq)
+            start_g(s, 1, AHEAD + 1)
+
+            @pl.loop(1, n_seq - AHEAD)
+            def _(j):
+                in_copy(last, partner(n_seq - j), me).wait_send()
+                g_copy(s, n_seq - AHEAD - j).start()
+
+            @pl.loop(n_seq - AHEAD, n_seq)
+            def _(j):
+                in_copy(last, partner(n_seq - j), me).wait_send()
+
             g_own(s).start()
 
-    mine = jnp.zeros((8, HD), F32)
+    mine = jnp.zeros((1, HD), F32)
     for s in range(samples):
         bucket = bucket_ref[s]
         total = jnp.sum(jnp.sum(loss_acc[s], axis=0, keepdims=True), axis=1, keepdims=True)
@@ -382,7 +390,7 @@
             device_id_type=MESH,
         ).wait_recv()
 
-    buckets = jnp.sum(loss_seq[...], axis=0)[0:1, :]
+    buckets = jnp.sum(loss_seq[...], axis=0)
     sum_loss = jnp.sum(jnp.where(lane < NB, buckets, 0.0), axis=1, keepdims=True)
     sum_count = jnp.sum(
         jnp.where((lane >= NB) & (lane < 2 * NB), buckets, 0.0), axis=1, keepdims=True
@@ -398,7 +406,9 @@
         weight = mean_all / (chosen_loss / chosen_count + 1e-5)
         turn_ref[s, 0] = weight * tables[s, 0]
         turn_ref[s, 1] = -weight * tables[s, 1]
-        weighed_ref[s] = weight * upright[s]
+        weighed = weight * upright[s]
+        for g in range(n_seq // GROUP):
+            weighed_ref[s, g] = weighed[:, g * GROUP : (g + 1) * GROUP]
 
     results = (
         pltpu.make_async_copy(turn_ref, turn_hbm, side_sem.at[0]),
@@ -452,70 +462,65 @@
     side_sem,
     out_sem,
 ):
-    samples, heads, _, rows, _ = grad_ref.shape
-    part = 16
-    pieces = 4
-    each = heads // pieces
-
-    def load(s, p):
-        some = pl.ds(p * each, each)
+    samples, heads = grad_ref.shape[:2]
+    groups = heads // GROUP
+
+    def load(s, g):
+        some = pl.ds(g * GROUP, GROUP)
         return pltpu.make_async_copy(
-            grad_hbm.at[s, some], grad_ref.at[s, some], grad_sem.at[s, p]
+            grad_hbm.at[s, some], grad_ref.at[s, some], grad_sem.at[s, g]
+        )
+
+    def store(s, g, array):
+        some = pl.ds(pl.multiple_of(g * (GROUP * HD), GROUP * HD), GROUP * HD)
+        return pltpu.make_async_copy(
+            out_ref.at[array, s, :, some],
+            (oq_hbm, ok_hbm, ov_hbm)[array].at[s, :, some],
+            out_sem.at[array, s, g],
         )
 
     side = (
         pltpu.make_async_copy(turn_hbm, turn_ref, side_sem.at[0]),
         pltpu.make_async_copy(weighed_hbm, weighed_ref, side_sem.at[1]),
     )
-
-    def store(s, r, array):
-        some = pl.ds(pl.multiple_of(r * part, part), part)
-        return pltpu.make_async_copy(
-            out_ref.at[array, s, some],
-            (oq_hbm, ok_hbm, ov_hbm)[array].at[s, some],
-            out_sem.at[array, s, r],
-        )
-
-    for p in range(pieces):
-        load(0, p).start()
     for copy in side:
         copy.start()
-    for s in range(1, samples):
-        for p in range(pieces):
-            load(s, p).start()
+
+    @pl.loop(0, samples * groups)
+    def _(i):
+        load(i // groups, i % groups).start()
+
     for copy in side:
         copy.wait()
 
-    @pl.loop(0, samples)
-    def _(s):
-        for p in range(pieces):
-            load(s, p).wait()
-
-        @pl.loop(0, rows // part)
-        def _(r):
-            some = pl.ds(pl.multiple_of(r * part, part), part)
-            for array in range(2):
-                turned = turn(
-                    [grad_ref[s, h, array, some] for h in range(heads)],
-                    turn_ref[s, 0, some],
-                    turn_ref[s, 1, some],
-                )
-                for h in range(heads):
-                    out_ref[array, s, some, h * HD : (h + 1) * HD] = turned[h]
-                store(s, r, array).start()
-            scales = weighed_ref[s, some]
-            for h in range(heads):
-                out_ref[2, s, some, h * HD : (h + 1) * HD] = (
-                    grad_ref[s, h, 2, some].astype(F32) * scales[:, h : h + 1]
-                ).astype(BF16)
-            store(s, r, 2).start()
-
-    @pl.loop(0, samples)
-    def _(s):
-        @pl.loop(0, rows // part)
-        def _(r):
-            for array in range(3):
-                store(s, r, array).wait()
+    @pl.loop(0, samples * groups)
+    def _(i):
+        s, g = i // groups, i % groups
+        load(s, g).wait()
+
+        def columns(h):
+            return pl.ds(pl.multiple_of((g * GROUP + h) * HD, HD), HD)
+
+        for array in range(2):
+            turned = turn(
+                [grad_ref[s, g * GROUP + h, array] for h in range(GROUP)],
+                turn_ref[s, 0],
+                turn_ref[s, 1],
+            )
+            for h in range(GROUP):
+                out_ref[array, s, :, columns(h)] = turned[h]
+            store(s, g, array).start()
+        scales = weighed_ref[s, g]
+        for h in range(GROUP):
+            out_ref[2, s, :, columns(h)] = (
+                grad_ref[s, g * GROUP + h, 2].astype(F32) * scales[:, h : h + 1]
+            ).astype(BF16)
+        store(s, g, 2).start()
+
+    @pl.loop(0, samples * groups)
+    def _(i):
+        for array in range(3):
+            store(i // groups, i % groups, array).wait()
 
 
 def local(n_dp, n_seq, q, k, v, scales, targets, frame_ids, bucket_ids):
@@ -532,7 +537,7 @@
         out_shape=(
             jax.ShapeDtypeStruct((samples, n_seq, 3, rows, HD), BF16),
             jax.ShapeDtypeStruct((samples, 2, rows, HD), F32),
-            jax.ShapeDtypeStruct((samples, rows, n_seq), F32),
+            jax.ShapeDtypeStruct((samples, n_seq // GROUP, rows, GROUP), F32),
         ),
         in_specs=[anywhere] * 7 + [smem],
         out_specs=(anywhere, anywhere, anywhere),
@@ -541,7 +546,7 @@
             pltpu.VMEM(frame_ids.shape, jnp.int32),
             pltpu.VMEM(freq.shape, F32),
             pltpu.VMEM((samples, 2, rows, HD), F32),
-            pltpu.VMEM((samples, rows, n_seq), F32),
+            pltpu.VMEM((samples, n_seq // GROUP, rows, GROUP), F32),
             pltpu.VMEM((samples, 3, rows, width), BF16),
             pltpu.VMEM((samples, 2, rows, HD), F32),
             pltpu.VMEM((samples, rows, n_seq), F32),
@@ -552,10 +557,10 @@
             pltpu.VMEM((LEN, HD), F32),
             pltpu.VMEM((LEN, HD), F32),
             pltpu.VMEM((samples, 8, HD), F32),
-            pltpu.VMEM((8, HD), F32),
-            pltpu.VMEM((n_dp, 8, HD), F32),
-            pltpu.VMEM((8, HD), F32),
-            pltpu.VMEM((n_seq, 8, HD), F32),
+            pltpu.VMEM((1, HD), F32),
+            pltpu.VMEM((n_dp, 1, HD), F32),
+            pltpu.VMEM((1, HD), F32),
+            pltpu.VMEM((n_seq, 1, HD), F32),
             dma((samples, n_seq)),
             dma((samples, n_seq)),
             dma((samples, n_seq)),
@@ -586,9 +591,9 @@
                 pltpu.VMEM(turns.shape, F32),
                 pltpu.VMEM(weighed.shape, F32),
                 pltpu.VMEM((3,) + q.shape, BF16),
-                dma((samples, 4)),
+                dma((samples, n_seq // GROUP)),
                 dma((2,)),
-                dma((3, samples, 4)),
+                dma((3, samples, n_seq // GROUP)),
             ],
             compiler_params=pltpu.CompilerParams(vmem_limit_bytes=58 << 20),
         )(grads, turns, weighed)

time: 189 us -> 184 us (0.974)
  Pallas kernels: 188 us -> 183 us
    pallas_call x1, Pallas kernels: 183 us -> 178 us  [local(): pl.pallas_call(functools.partial(kernel, n_dp, n_seq), out_shape=(jax.Sha...]
where the time goes in v4:
time: 184 us; the launch traced here: 183 us
  Pallas kernels  183 us (99%)
    pallas_call x1, Pallas kernels, local(): pl.pallas_call(functools.partial(kernel, n_dp, n_seq), out_shape=(jax.Sha...  178 us
    pallas_call x1, Pallas kernels, local(): pl.pallas_call(finish, out_shape=(out, out, out), in_specs=[anywhere] * 3...  4.34 us

profile of v4, /device:TPU:1, one launch (start us, length us, event | category | flops | bytes accessed | tf_op | source)
XLA Modules:
  0.0 183.3 jit_solution(4192236809156131901)
XLA Ops:
  0.6 178.3 %shard_map.103 = (bf16[2,32,3,64,128]{4,3,2,1,0:T(8,128)(2,1)}, f32[2,2,64,128]{3,2,1,0:T(8,128)}, f32[2,4,64,8]{3,2,1,0:T(8,128)}) custom-call(bf16[2,64,4096]{2,1,0:T(8,128)(2,1)} %q_ref.1, bf16[2,64,4096]{2,1,0:T(8,128)(2,1)} %k_ref.1, bf16[2,64,4096]{2,1,0:T(8,128)(2,1)} %v_ref.1, bf16[2,64,4096]{2,1,0:T(8,128)(2,1)} %t_ref.1, f32[2,32,64]{2,1,0:T(8,128)} %bitcast.1, ...), custom_call_target="tpu_custom_call" | custom-call | tf_op jit(solution)/shard_map/pallas_call | solution.py:535
  179.0 4.3 %shard_map.104 = (bf16[2,64,4096]{2,1,0:T(8,128)(2,1)}, bf16[2,64,4096]{2,1,0:T(8,128)(2,1)}, bf16[2,64,4096]{2,1,0:T(8,128)(2,1)}) custom-call(bf16[2,32,3,64,128]{4,3,2,1,0:T(8,128)(2,1)} %get-tuple-element.6.grad_hbm, f32[2,2,64,128]{3,2,1,0:T(8,128)} %get-tuple-element.7.turn_hbm, f32[2,4,64,8]{3,2,1,0:T(8,128)} %get-tuple-element.8.weighed_hbm), custom_call_target="tpu_custom_call" | custom-call | tf_op jit(solution)/shard_map/pallas_call | solution.py:584

commit v5 on v4

--- a/solution.py
+++ b/solution.py
@@ -92,10 +92,10 @@
     my_z, my_y = me // YS, me % YS
 
     def partner(i):
-        a, dy = i // YS, i % YS
+        a, dy = i % ZS, i // ZS
         half = (a + 1) // 2
         dz = half * (1 - 2 * (a % 2)) + ZS
-        return ((my_z + dz) % ZS) * YS + (my_y + dy) % YS
+        return ((my_z + dz) % ZS) * YS + (my_y + dy + half) % YS
 
     barrier = pltpu.get_barrier_semaphore()
 
@@ -206,10 +206,6 @@
             own_sem.at[1, s],
         )
 
-    def plane(a):
-        half = (ZS - a) // 2
-        return (my_z + half * (1 - 2 * ((ZS - 1 - a) % 2)) + ZS) % ZS
-
     def prepare(s, z):
         def block(array, y):
             return held[s, array, :, pl.ds(pl.multiple_of((z * YS + y) * HD, HD), HD)]
@@ -223,17 +219,6 @@
             send_in[s, head, 0] = turned[y]
             send_in[s, head, 1] = turned[YS + y]
             send_in[s, head, 2] = (block(2, y).astype(F32) * scales[:, y : y + 1]).astype(BF16)
-
-    def send(s, z):
-        for y in range(YS):
-            to = z * YS + y
-
-            @pl.when(to != me)
-            def _():
-                if s > 0:
-                    in_copy(s - 1, to, me).wait_send()
-                    t_copy(s, to, me).start()
-                in_copy(s, to, me).start()
 
     def attend(s):
         grad_k[...] = jnp.zeros_like(grad_k)
@@ -287,14 +272,27 @@
     for s in range(samples):
         ready_tables(s)
         t_own(s).start()
-    for s in range(samples):
         for array in range(3):
             load(s, array).wait()
 
         @pl.loop(0, ZS)
-        def _(a):
-            prepare(s, plane(a))
-            send(s, plane(a))
+        def _(z):
+            prepare(s, z)
+
+        if s == 0:
+
+            @pl.loop(1, n_seq)
+            def _(j):
+                in_copy(s, partner(n_seq - j), me).start()
+
+        else:
+
+            @pl.loop(1, n_seq)
+            def _(j):
+                to = partner(n_seq - j)
+                in_copy(s - 1, to, me).wait_send()
+                t_copy(s, to, me).start()
+                in_copy(s, to, me).start()
 
         in_own(s).start()
 
@@ -501,14 +499,14 @@
         def columns(h):
             return pl.ds(pl.multiple_of((g * GROUP + h) * HD, HD), HD)
 
+        turned = turn(
+            [grad_ref[s, g * GROUP + h, array] for array in range(2) for h in range(GROUP)],
+            turn_ref[s, 0],
+            turn_ref[s, 1],
+        )
         for array in range(2):
-            turned = turn(
-                [grad_ref[s, g * GROUP + h, array] for h in range(GROUP)],
-                turn_ref[s, 0],
-                turn_ref[s, 1],
-            )
             for h in range(GROUP):
-                out_ref[array, s, :, columns(h)] = turned[h]
+                out_ref[array, s, :, columns(h)] = turned[array * GROUP + h]
             store(s, g, array).start()
         scales = weighed_ref[s, g]
         for h in range(GROUP):

time: 184 us -> 182 us (0.989)
  no operation moved by 1% of the time
where the time goes in v5:
time: 182 us
  Pallas kernels  182 us (100%)
    pallas_call x1, Pallas kernels, local(): pl.pallas_call(functools.partial(kernel, n_dp, n_seq), out_shape=(jax.Sha...  177 us
    pallas_call x1, Pallas kernels, local(): pl.pallas_call(finish, out_shape=(out, out, out), in_specs=[anywhere] * 3...  4.34 us

profile of v5, /device:TPU:1, one launch (start us, length us, event | category | flops | bytes accessed | tf_op | source)
XLA Modules:
  0.0 182.2 jit_solution(9533702510331914945)
XLA Ops:
  0.6 177.2 %shard_map.103 = (bf16[2,32,3,64,128]{4,3,2,1,0:T(8,128)(2,1)}, f32[2,2,64,128]{3,2,1,0:T(8,128)}, f32[2,4,64,8]{3,2,1,0:T(8,128)}) custom-call(bf16[2,64,4096]{2,1,0:T(8,128)(2,1)} %q_ref.1, bf16[2,64,4096]{2,1,0:T(8,128)(2,1)} %k_ref.1, bf16[2,64,4096]{2,1,0:T(8,128)(2,1)} %v_ref.1, bf16[2,64,4096]{2,1,0:T(8,128)(2,1)} %t_ref.1, f32[2,32,64]{2,1,0:T(8,128)} %bitcast.1, ...), custom_call_target="tpu_custom_call" | custom-call | tf_op jit(solution)/shard_map/pallas_call | solution.py:533
  177.9 4.3 %shard_map.104 = (bf16[2,64,4096]{2,1,0:T(8,128)(2,1)}, bf16[2,64,4096]{2,1,0:T(8,128)(2,1)}, bf16[2,64,4096]{2,1,0:T(8,128)(2,1)}) custom-call(bf16[2,32,3,64,128]{4,3,2,1,0:T(8,128)(2,1)} %get-tuple-element.6.grad_hbm, f32[2,2,64,128]{3,2,1,0:T(8,128)} %get-tuple-element.7.turn_hbm, f32[2,4,64,8]{3,2,1,0:T(8,128)} %get-tuple-element.8.weighed_hbm), custom_call_target="tpu_custom_call" | custom-call | tf_op jit(solution)/shard_map/pallas_call | solution.py:582

commit v6 on v5

--- a/solution.py
+++ b/solution.py
@@ -92,7 +92,7 @@
     my_z, my_y = me // YS, me % YS
 
     def partner(i):
-        a, dy = i % ZS, i // ZS
+        a, dy = i % ZS * 3 % ZS, i // ZS
         half = (a + 1) // 2
         dz = half * (1 - 2 * (a % 2)) + ZS
         return ((my_z + dz) % ZS) * YS + (my_y + dy + half) % YS

time: 182 us -> 181 us (level)
  Pallas kernels: 182 us -> 180 us
where the time goes in v6:
time: 181 us
  Pallas kernels  180 us (99%)
    pallas_call x1, Pallas kernels, local(): pl.pallas_call(functools.partial(kernel, n_dp, n_seq), out_shape=(jax.Sha...  176 us
    pallas_call x1, Pallas kernels, local(): pl.pallas_call(finish, out_shape=(out, out, out), in_specs=[anywhere] * 3...  4.34 us

profile of v6, /device:TPU:1, one launch (start us, length us, event | category | flops | bytes accessed | tf_op | source)
XLA Modules:
  0.0 181.0 jit_solution(12932299417889127602)
XLA Ops:
  0.6 176.0 %shard_map.103 = (bf16[2,32,3,64,128]{4,3,2,1,0:T(8,128)(2,1)}, f32[2,2,64,128]{3,2,1,0:T(8,128)}, f32[2,4,64,8]{3,2,1,0:T(8,128)}) custom-call(bf16[2,64,4096]{2,1,0:T(8,128)(2,1)} %q_ref.1, bf16[2,64,4096]{2,1,0:T(8,128)(2,1)} %k_ref.1, bf16[2,64,4096]{2,1,0:T(8,128)(2,1)} %v_ref.1, bf16[2,64,4096]{2,1,0:T(8,128)(2,1)} %t_ref.1, f32[2,32,64]{2,1,0:T(8,128)} %bitcast.1, ...), custom_call_target="tpu_custom_call" | custom-call | tf_op jit(solution)/shard_map/pallas_call | solution.py:533
  176.6 4.3 %shard_map.104 = (bf16[2,64,4096]{2,1,0:T(8,128)(2,1)}, bf16[2,64,4096]{2,1,0:T(8,128)(2,1)}, bf16[2,64,4096]{2,1,0:T(8,128)(2,1)}) custom-call(bf16[2,32,3,64,128]{4,3,2,1,0:T(8,128)(2,1)} %get-tuple-element.6.grad_hbm, f32[2,2,64,128]{3,2,1,0:T(8,128)} %get-tuple-element.7.turn_hbm, f32[2,4,64,8]{3,2,1,0:T(8,128)} %get-tuple-element.8.weighed_hbm), custom_call_target="tpu_custom_call" | custom-call | tf_op jit(solution)/shard_map/pallas_call | solution.py:582

commit v7 on v6

--- a/solution.py
+++ b/solution.py
@@ -36,6 +36,19 @@
     shape = (len(blocks),) + blocks[0].shape
     turned = x.astype(F32).reshape(shape) * cosine + swapped.reshape(shape) * sine
     return turned.astype(BF16)
+
+
+def turn_back(grad_ref, g, tables, scales, out_ref):
+    turned = turn(
+        [grad_ref[g * GROUP + h, array] for array in range(2) for h in range(GROUP)], *tables
+    )
+    for h in range(GROUP):
+        columns = pl.ds(pl.multiple_of((g * GROUP + h) * HD, HD), HD)
+        for array in range(2):
+            out_ref[array, :, columns] = turned[array * GROUP + h]
+        out_ref[2, :, columns] = (
+            grad_ref[g * GROUP + h, 2].astype(F32) * scales[:, h : h + 1]
+        ).astype(BF16)
 
 
 def kernel(
@@ -52,11 +65,14 @@
     recv_g,
     turn_hbm,
     weighed_hbm,
+    done_hbm,
     scale_ref,
     frame_ref,
     freq_ref,
     turn_ref,
     weighed_ref,
+    first_g,
+    done_ref,
     held,
     tables,
     upright,
@@ -192,7 +208,7 @@
         to = partner(i)
         return pltpu.make_async_remote_copy(
             src_ref=send_g.at[s, :, pl.ds(pl.multiple_of(to * rows, rows), rows), :],
-            dst_ref=recv_g.at[s, me],
+            dst_ref=(recv_g if s == last else first_g).at[me],
             send_sem=g_send.at[s, i],
             recv_sem=g_recv.at[s, me],
             device_id=(dp, to),
@@ -202,7 +218,7 @@
     def g_own(s):
         return pltpu.make_async_copy(
             send_g.at[s, :, pl.ds(pl.multiple_of(me * rows, rows), rows), :],
-            recv_g.at[s, me],
+            (recv_g if s == last else first_g).at[me],
             own_sem.at[1, s],
         )
 
@@ -303,18 +319,18 @@
 
         @pl.when(s < last)
         def _():
-            start_g(s, 1, AHEAD + 1)
+            start_g(0, 1, AHEAD + 1)
 
             @pl.loop(1, n_seq - AHEAD)
             def _(j):
                 in_copy(last, partner(n_seq - j), me).wait_send()
-                g_copy(s, n_seq - AHEAD - j).start()
+                g_copy(0, n_seq - AHEAD - j).start()
 
             @pl.loop(n_seq - AHEAD, n_seq)
             def _(j):
                 in_copy(last, partner(n_seq - j), me).wait_send()
 
-            g_own(s).start()
+            g_own(0).start()
 
     mine = jnp.zeros((1, HD), F32)
     for s in range(samples):
@@ -409,8 +425,8 @@
             weighed_ref[s, g] = weighed[:, g * GROUP : (g + 1) * GROUP]
 
     results = (
-        pltpu.make_async_copy(turn_ref, turn_hbm, side_sem.at[0]),
-        pltpu.make_async_copy(weighed_ref, weighed_hbm, side_sem.at[1]),
+        pltpu.make_async_copy(turn_ref.at[last], turn_hbm, side_sem.at[0]),
+        pltpu.make_async_copy(weighed_ref.at[last], weighed_hbm, side_sem.at[1]),
     )
     for copy in results:
         copy.start()
@@ -423,13 +439,24 @@
             src = (me + i) % n_seq
             pltpu.make_async_remote_copy(
                 src_ref=send_g.at[s, :, pl.ds(pl.multiple_of(src * rows, rows), rows), :],
-                dst_ref=recv_g.at[s, src],
+                dst_ref=(recv_g if s == last else first_g).at[src],
                 send_sem=g_send.at[s, i],
                 recv_sem=g_recv.at[s, src],
                 device_id=(dp, src),
                 device_id_type=MESH,
             ).wait_recv()
 
+        if s == 0:
+
+            @pl.loop(0, n_seq // GROUP)
+            def _(g):
+                turn_back(
+                    first_g, g, (turn_ref[0, 0], turn_ref[0, 1]), weighed_ref[0, g], done_ref
+                )
+
+            done = pltpu.make_async_copy(done_ref, done_hbm, side_sem.at[2])
+            done.start()
+
     @pl.loop(1, n_seq)
     def _(i):
         for s in range(samples):
@@ -441,7 +468,7 @@
     def _(i):
         dp_copy(i).wait_send()
 
-    for copy in results:
+    for copy in (*results, done):
         copy.wait()
 
 
@@ -449,6 +476,7 @@
     grad_hbm,
     turn_hbm,
     weighed_hbm,
+    done_hbm,
     oq_hbm,
     ok_hbm,
     ov_hbm,
@@ -456,69 +484,71 @@
     turn_ref,
     weighed_ref,
     out_ref,
+    done_ref,
     grad_sem,
     side_sem,
     out_sem,
+    done_sem,
 ):
-    samples, heads = grad_ref.shape[:2]
-    groups = heads // GROUP
-
-    def load(s, g):
+    groups = grad_ref.shape[0] // GROUP
+    last = oq_hbm.shape[0] - 1
+    outs = (oq_hbm, ok_hbm, ov_hbm)
+
+    def load(g):
         some = pl.ds(g * GROUP, GROUP)
-        return pltpu.make_async_copy(
-            grad_hbm.at[s, some], grad_ref.at[s, some], grad_sem.at[s, g]
-        )
-
-    def store(s, g, array):
+        return pltpu.make_async_copy(grad_hbm.at[some], grad_ref.at[some], grad_sem.at[g])
+
+    def store(g, array):
         some = pl.ds(pl.multiple_of(g * (GROUP * HD), GROUP * HD), GROUP * HD)
         return pltpu.make_async_copy(
-            out_ref.at[array, s, :, some],
-            (oq_hbm, ok_hbm, ov_hbm)[array].at[s, :, some],
-            out_sem.at[array, s, g],
+            out_ref.at[array, :, some], outs[array].at[last, :, some], out_sem.at[array, g]
         )
 
     side = (
         pltpu.make_async_copy(turn_hbm, turn_ref, side_sem.at[0]),
         pltpu.make_async_copy(weighed_hbm, weighed_ref, side_sem.at[1]),
     )
+    done_in = [
+        pltpu.make_async_copy(done_hbm.at[array], done_ref.at[array], done_sem.at[0, array])
+        for array in range(3)
+    ]
+    done_out = [
+        pltpu.make_async_copy(done_ref.at[array], outs[array].at[0], done_sem.at[1, array])
+        for array in range(3)
+    ]
+    load(0).start()
     for copy in side:
         copy.start()
 
-    @pl.loop(0, samples * groups)
-    def _(i):
-        load(i // groups, i % groups).start()
-
+    @pl.loop(1, groups)
+    def _(g):
+        load(g).start()
+
+    for copy in done_in:
+        copy.start()
     for copy in side:
         copy.wait()
 
-    @pl.loop(0, samples * groups)
-    def _(i):
-        s, g = i // groups, i % groups
-        load(s, g).wait()
-
-        def columns(h):
-            return pl.ds(pl.multiple_of((g * GROUP + h) * HD, HD), HD)
-
-        turned = turn(
-            [grad_ref[s, g * GROUP + h, array] for array in range(2) for h in range(GROUP)],
-            turn_ref[s, 0],
-            turn_ref[s, 1],
-        )
-        for array in range(2):
-            for h in range(GROUP):
-                out_ref[array, s, :, columns(h)] = turned[array * GROUP + h]
-            store(s, g, array).start()
-        scales = weighed_ref[s, g]
-        for h in range(GROUP):
-            out_ref[2, s, :, columns(h)] = (
-                grad_ref[s, g * GROUP + h, 2].astype(F32) * scales[:, h : h + 1]
-            ).astype(BF16)
-        store(s, g, 2).start()
-
-    @pl.loop(0, samples * groups)
-    def _(i):
+    @pl.loop(0, groups)
+    def _(g):
+        load(g).wait()
+        turn_back(grad_ref, g, (turn_ref[0], turn_ref[1]), weighed_ref[g], out_ref)
         for array in range(3):
-            store(i // groups, i % groups, array).wait()
+            store(g, array).start()
+
+        @pl.when(g == 0)
+        def _():
+            for array in range(3):
+                done_in[array].wait()
+                done_out[array].start()
+
+    @pl.loop(0, groups)
+    def _(g):
+        for array in range(3):
+            store(g, array).wait()
+
+    for copy in done_out:
+        copy.wait()
 
 
 def local(n_dp, n_seq, q, k, v, scales, targets, frame_ids, bucket_ids):
@@ -530,21 +560,24 @@
     smem = pl.BlockSpec(memory_space=pltpu.SMEM)
     anywhere = pl.BlockSpec(memory_space=pl.ANY)
     dma = pltpu.SemaphoreType.DMA
-    grads, turns, weighed = pl.pallas_call(
+    grads, turns, weighed, done = pl.pallas_call(
         functools.partial(kernel, n_dp, n_seq),
         out_shape=(
-            jax.ShapeDtypeStruct((samples, n_seq, 3, rows, HD), BF16),
-            jax.ShapeDtypeStruct((samples, 2, rows, HD), F32),
-            jax.ShapeDtypeStruct((samples, n_seq // GROUP, rows, GROUP), F32),
+            jax.ShapeDtypeStruct((n_seq, 3, rows, HD), BF16),
+            jax.ShapeDtypeStruct((2, rows, HD), F32),
+            jax.ShapeDtypeStruct((n_seq // GROUP, rows, GROUP), F32),
+            jax.ShapeDtypeStruct((3, rows, width), BF16),
         ),
         in_specs=[anywhere] * 7 + [smem],
-        out_specs=(anywhere, anywhere, anywhere),
+        out_specs=(anywhere,) * 4,
         scratch_shapes=[
             pltpu.VMEM(scales.shape, F32),
             pltpu.VMEM(frame_ids.shape, jnp.int32),
             pltpu.VMEM(freq.shape, F32),
             pltpu.VMEM((samples, 2, rows, HD), F32),
             pltpu.VMEM((samples, n_seq // GROUP, rows, GROUP), F32),
+            pltpu.VMEM((n_seq, 3, rows, HD), BF16),
+            pltpu.VMEM((3, rows, width), BF16),
             pltpu.VMEM((samples, 3, rows, width), BF16),
             pltpu.VMEM((samples, 2, rows, HD), F32),
             pltpu.VMEM((samples, rows, n_seq), F32),
@@ -582,19 +615,21 @@
         pl.pallas_call(
             finish,
             out_shape=(out, out, out),
-            in_specs=[anywhere] * 3,
+            in_specs=[anywhere] * 4,
             out_specs=(anywhere,) * 3,
             scratch_shapes=[
                 pltpu.VMEM(grads.shape, BF16),
                 pltpu.VMEM(turns.shape, F32),
                 pltpu.VMEM(weighed.shape, F32),
-                pltpu.VMEM((3,) + q.shape, BF16),
-                dma((samples, n_seq // GROUP)),
+                pltpu.VMEM(done.shape, BF16),
+                pltpu.VMEM(done.shape, BF16),
+                dma((n_seq // GROUP,)),
                 dma((2,)),
-                dma((3, samples, n_seq // GROUP)),
+                dma((3, n_seq // GROUP)),
+                dma((2, 3)),
             ],
             compiler_params=pltpu.CompilerParams(vmem_limit_bytes=58 << 20),
-        )(grads, turns, weighed)
+        )(grads, turns, weighed, done)
     )
 
 

time: 181 us -> 181 us (level)
  no operation moved by 1% of the time
where the time goes in v7:
time: 181 us; the launch traced here: 180 us
  Pallas kernels  180 us (99%)
    pallas_call x1, Pallas kernels, local(): pl.pallas_call(functools.partial(kernel, n_dp, n_seq), out_shape=(jax.Sha...  176 us
    pallas_call x1, Pallas kernels, local(): pl.pallas_call(finish, out_shape=(out, out, out), in_specs=[anywhere] * 4...  3.71 us

profile of v7, /device:TPU:1, one launch (start us, length us, event | category | flops | bytes accessed | tf_op | source)
XLA Modules:
  0.0 180.3 jit_solution(7276310198215468796)
XLA Ops:
  0.6 176.0 %shard_map.103 = (bf16[32,3,64,128]{3,2,1,0:T(8,128)(2,1)}, f32[2,64,128]{2,1,0:T(8,128)}, f32[4,64,8]{2,1,0:T(8,128)}, bf16[3,64,4096]{2,1,0:T(8,128)(2,1)}) custom-call(bf16[2,64,4096]{2,1,0:T(8,128)(2,1)} %q_ref.1, bf16[2,64,4096]{2,1,0:T(8,128)(2,1)} %k_ref.1, bf16[2,64,4096]{2,1,0:T(8,128)(2,1)} %v_ref.1, bf16[2,64,4096]{2,1,0:T(8,128)(2,1)} %t_ref.1, ...), custom_call_target="tpu_custom_call" | custom-call | tf_op jit(solution)/shard_map/pallas_call | solution.py:563
  176.6 3.7 %shard_map.104 = (bf16[2,64,4096]{2,1,0:T(8,128)(2,1)}, bf16[2,64,4096]{2,1,0:T(8,128)(2,1)}, bf16[2,64,4096]{2,1,0:T(8,128)(2,1)}) custom-call(bf16[32,3,64,128]{3,2,1,0:T(8,128)(2,1)} %get-tuple-element.7.grad_hbm, f32[2,64,128]{2,1,0:T(8,128)} %get-tuple-element.8.turn_hbm, f32[4,64,8]{2,1,0:T(8,128)} %get-tuple-element.9.weighed_hbm, ...), custom_call_target="tpu_custom_call" | custom-call | tf_op jit(solution)/shard_map/pallas_call | solution.py:615
